TPU v7x, 512 devices: a whole 4x8x8 slice. The times are simulated.
512 devices in a mesh: blk: 32 (over y_hi, x, core), expert: 16 (over y_lo, z).
Axes of the slice: x: 4, y: 8 (y_hi: 4, y_lo: 2; y = y_hi * 2 + y_lo), z: 8, core: 2. Of those that a mesh axis runs over, the one named last changes fastest.
Arguments:
- queries: bfloat16 [16, 72, 4096], P('expert', None, 'blk'), may hold values from -6 to 6
- keys: bfloat16 [16, 72, 4096], P('expert', None, 'blk'), may hold values from -6 to 6
- values: bfloat16 [16, 72, 4096], P('expert', None, 'blk'), may hold values from -24 to 24
- image_ids: int32 [1024], P('blk'), may hold values from 0 to 2, as said below
- placement: int32 [1024, 1], P('blk'), may hold values from 0 to 31; in each aligned block of 32 rows (0 to 31, 32 to 63, ...) at most 4 rows name the same one
- merge_gain: float32 [16, 288], P('expert'), may hold values from 0.1 to 1.9
- merge_weight: bfloat16 [16, 288, 2048], P('expert'), may hold values from -0.09375 to 0.09375
- text: bfloat16 [4096, 2048], P('blk'), may hold values from -6 to 6
- norm_gain: float32 [2048], replicated, may hold values from 0.1 to 1.9
- w_gate: bfloat16 [32, 3072, 2048], P('blk', 'expert'), may hold values from -0.125 to 0.125
- w_up: bfloat16 [32, 3072, 2048], P('blk', 'expert'), may hold values from -0.125 to 0.125
- w_down: bfloat16 [32, 3072, 2048], P('blk', 'expert'), may hold values from -0.15625 to 0.15625
- routes: int32 [4096, 8], P('blk'), may hold values from 0 to 127, all different within a row; in each aligned block of 128 rows (0 to 127, 128 to 255, ...) at most 10 rows name the same one
- route_gates: float32 [4096, 8], P('blk'), may hold values from 0.2 to 1
- cotangent: bfloat16 [4096, 2048], P('blk'), may hold values from -6 to 6
Outputs:
- llm_out: bfloat16 [4096, 2048], P('blk')
- attn_grad: float32 [16, 72, 4096], P('expert', None, 'blk')
Inputs may be any that keep to these rules, and one draw needn't show every extreme that they name: `image_ids`: three images in order: ids never fall along the sequence; image 0 holds from 64 to 127 merged rows and image 2 from 65 to 128. `placement`: among the 32 rows of one encoder index no shard is named more than 4 times. `routes`: each token names 8 different experts; among the 128 tokens of one shard no expert is named more than 10 times.
All inputs are finite; a program needn't handle non-finite values.
Results may differ from a plain program's by a relative error of at most 0.03.
Values may be sent and summed in bfloat16 or wider, within the bound.
A program may use at most 64 MiB of HBM per device.

v0:
```python
import jax
import jax.numpy as jnp
from jax import lax
from jax.sharding import PartitionSpec as P

CAPX = 10


EPS = 1e-06


def block_ranks(hit_table):
    before = jnp.cumsum(hit_table, axis=0) - hit_table
    return jnp.sum(before * hit_table, axis=1)


def body(
    queries,
    keys,
    values,
    image_ids,
    placement,
    merge_gain,
    merge_weight,
    text,
    norm_gain,
    w_gate,
    w_up,
    w_down,
    routes,
    route_gates,
    cotangent,
):
    blocks = lax.axis_size("blk")
    my_index = lax.axis_index("blk")
    expert_size = lax.axis_size("expert")
    expert_index = lax.axis_index("expert")
    heads_here, head_size, patches = queries.shape
    merged_rows = image_ids.shape[0]
    llm_rows, model_width = text.shape
    top_count = routes.shape[1]
    along_width = (((1,), (1,)), ((), ()))
    all_ids, all_dest = (
        lax.all_gather(image_ids, "blk", axis=0, tiled=True),
        lax.all_gather(placement[:, 0], "blk", axis=0, tiled=True),
    )
    patch_ids = jnp.repeat(all_ids, 4)
    my_ids = lax.dynamic_slice_in_dim(patch_ids, my_index * patches, patches, 0)
    score_scale = head_size ** (-0.5)
    run_max = jnp.full((heads_here, patches), -1e30, jnp.float32)
    key_part = lax.all_gather(keys, "blk", axis=2, tiled=True)
    value_part = lax.all_gather(values, "blk", axis=2, tiled=True)
    scores = (
        jnp.einsum("hdq,hdk->hqk", queries, key_part, preferred_element_type=jnp.float32)
        * score_scale
    )
    scores = jnp.where((my_ids[:, None] == patch_ids[None, :])[None], scores, -1e30)
    new_max = jnp.maximum(run_max, jnp.max(scores, axis=-1))
    weights = jnp.exp(scores - new_max[:, :, None])
    run_sum = jnp.sum(weights, axis=-1)
    weighted = jnp.einsum(
        "hqk,hdk->hdq", weights.astype(jnp.bfloat16), value_part, preferred_element_type=jnp.float32
    )
    run_max, run_sum, weighted = (new_max, run_sum, weighted)
    attn = (weighted / run_sum[:, None, :]).astype(jnp.bfloat16)
    spread = jnp.transpose(attn, (2, 0, 1)).reshape(merged_rows, 4, heads_here, head_size)
    merged = (
        jnp.transpose(spread, (0, 2, 1, 3))
        .reshape(merged_rows, heads_here * 4 * head_size)
        .astype(jnp.float32)
    )
    full_width = expert_size * merged.shape[1]
    row_sums, row_squares = lax.psum(
        (jnp.sum(merged, axis=1), jnp.sum(merged * merged, axis=1)), "expert"
    )
    row_mean = row_sums / full_width
    inv_std = lax.rsqrt(row_squares / full_width - row_mean * row_mean + EPS)
    normed = (merged - row_mean[:, None]) * inv_std[:, None]
    gain_flat = merge_gain.reshape(-1)
    scaled = (normed * gain_flat).astype(jnp.bfloat16)
    weight_flat = merge_weight.reshape(-1, merge_weight.shape[2])
    merger_part = jnp.dot(scaled, weight_flat, preferred_element_type=jnp.float32)
    vision = lax.psum(merger_part.astype(jnp.bfloat16), "expert")
    cap_rows = llm_rows // blocks
    long_rows = all_dest.shape[0]
    dest_hits = (all_dest[:, None] == jnp.arange(blocks, dtype=jnp.int32)[None, :]).astype(
        jnp.int32
    )
    slot_index = block_ranks(dest_hits)
    grouped = dest_hits.reshape(blocks, merged_rows, blocks)
    inner_before = jnp.cumsum(grouped, axis=1) - grouped
    block_rank = jnp.sum(inner_before * grouped, axis=2).reshape(long_rows)
    my_dest = lax.dynamic_slice_in_dim(all_dest, my_index * merged_rows, merged_rows, 0)
    local_rank = lax.dynamic_slice_in_dim(block_rank, my_index * merged_rows, merged_rows, 0)
    send_rows = (
        jnp.zeros((blocks, cap_rows, model_width), jnp.bfloat16).at[my_dest, local_rank].set(vision)
    )
    arrived = lax.all_to_all(send_rows, "blk", split_axis=0, concat_axis=0, tiled=True)
    source_block = jnp.arange(long_rows, dtype=jnp.int32) // merged_rows
    arrival = source_block * cap_rows + block_rank
    slot_target = jnp.where(all_dest == my_index, slot_index, llm_rows)
    slot_source = jnp.zeros((llm_rows,), jnp.int32).at[slot_target].set(arrival, mode="drop")
    slot_vision = jnp.zeros((llm_rows,), jnp.bool_).at[slot_target].set(True, mode="drop")
    flat_arrived = arrived.reshape(blocks * cap_rows, model_width)
    hidden_in = jnp.where(slot_vision[:, None], flat_arrived[slot_source], text)
    inputs_f32 = hidden_in.astype(jnp.float32)

    def rms_norm(inputs):
        return (
            inputs * lax.rsqrt(jnp.mean(inputs * inputs, axis=-1, keepdims=True) + EPS) * norm_gain
        )

    normed_h, norm_pull = jax.vjp(rms_norm, inputs_f32)
    h_rows = normed_h.astype(jnp.bfloat16)
    group_count = expert_size // 2
    member = expert_index // group_count
    window = 2 * blocks
    pair_expert = routes.reshape(-1)
    pair_hits = (pair_expert[:, None] == jnp.arange(window, dtype=jnp.int32)[None, :]).astype(
        jnp.int32
    )
    pair_rank = block_ranks(pair_hits)
    pair_live = (pair_expert < window) & (pair_expert % 2 == member)
    slot_count = blocks * CAPX
    pair_slot = jnp.where(pair_live, pair_expert // 2 * CAPX + pair_rank, slot_count)
    pair_token = jnp.arange(llm_rows * top_count, dtype=jnp.int32) // top_count
    pair_gate = jnp.where(pair_live, route_gates.reshape(-1), 0.0)
    slot_token = jnp.zeros((slot_count,), jnp.int32).at[pair_slot].set(pair_token, mode="drop")
    slot_gate = jnp.zeros((slot_count,), jnp.float32).at[pair_slot].set(pair_gate, mode="drop")
    slot_live = jnp.zeros((slot_count,), jnp.float32).at[pair_slot].set(1.0, mode="drop")

    def dispatch(slot_rows):
        buffer = jnp.where(slot_live[:, None] > 0.0, slot_rows, jnp.zeros_like(slot_rows))
        landed = lax.all_to_all(
            buffer.reshape(blocks, CAPX, model_width),
            "blk",
            split_axis=0,
            concat_axis=0,
            tiled=True,
        )
        return landed.reshape(slot_count, model_width)

    def combine(landed, slot_weight):
        weighted_rows = (
            landed.reshape(slot_count, model_width).astype(jnp.float32) * slot_weight[:, None]
        )
        return jnp.zeros((llm_rows, model_width), jnp.float32).at[slot_token].add(weighted_rows)

    def to_owner(partial_value, slot_weight):
        returned = lax.all_to_all(
            partial_value.astype(jnp.bfloat16).reshape(blocks, CAPX, model_width),
            "blk",
            split_axis=0,
            concat_axis=0,
            tiled=True,
        )
        combined = combine(returned, slot_weight)
        return lax.psum(combined.astype(jnp.bfloat16), "expert").astype(jnp.float32)

    gate_rows = w_gate[0]
    up_rows = w_up[0]
    down_rows = w_down[0]
    expert_rows = dispatch(h_rows[slot_token])
    gate_pre = lax.dot_general(
        expert_rows, gate_rows, along_width, preferred_element_type=jnp.float32
    )
    up_proj = lax.dot_general(expert_rows, up_rows, along_width, preferred_element_type=jnp.float32)
    activated = (jax.nn.silu(gate_pre) * up_proj).astype(jnp.bfloat16)
    down_part = jnp.dot(activated, down_rows, preferred_element_type=jnp.float32)
    expert_sum = to_owner(down_part, slot_gate)
    llm_out = (inputs_f32 + expert_sum).astype(jnp.bfloat16)
    cot_rows = cotangent.astype(jnp.float32)
    back_rows = dispatch((cot_rows[slot_token] * slot_gate[:, None]).astype(jnp.bfloat16))
    act_grad = lax.dot_general(
        back_rows, down_rows, along_width, preferred_element_type=jnp.float32
    )
    sigmoid_gate = jax.nn.sigmoid(gate_pre)
    gate_grad = (
        act_grad * up_proj * sigmoid_gate * (1.0 + gate_pre * (1.0 - sigmoid_gate))
    ).astype(jnp.bfloat16)
    up_grad = (act_grad * gate_pre * sigmoid_gate).astype(jnp.bfloat16)
    row_grad = jnp.dot(gate_grad, gate_rows, preferred_element_type=jnp.float32) + jnp.dot(
        up_grad, up_rows, preferred_element_type=jnp.float32
    )
    hidden_grad = to_owner(row_grad, slot_live)
    input_grad = (cot_rows + norm_pull(hidden_grad)[0]).astype(jnp.bfloat16)
    back_target = jnp.where(slot_vision, slot_source, blocks * cap_rows)
    grad_buffer = (
        jnp.zeros((blocks * cap_rows, model_width), jnp.bfloat16)
        .at[back_target]
        .set(input_grad, mode="drop")
    )
    returned_rows = lax.all_to_all(
        grad_buffer.reshape(blocks, cap_rows, model_width),
        "blk",
        split_axis=0,
        concat_axis=0,
        tiled=True,
    )
    vision_grad = returned_rows[my_dest, local_rank]
    scaled_grad = lax.dot_general(
        vision_grad, weight_flat, along_width, preferred_element_type=jnp.float32
    )
    normed_grad = scaled_grad * gain_flat
    grad_sum, cross_sum = lax.psum(
        (jnp.sum(normed_grad, axis=1), jnp.sum(normed_grad * normed, axis=1)), "expert"
    )
    merged_grad = inv_std[:, None] * (
        normed_grad - (grad_sum / full_width)[:, None] - normed * (cross_sum / full_width)[:, None]
    )
    unfolded = (
        merged_grad.reshape(merged_rows, heads_here, 4, head_size)
        .transpose(0, 2, 1, 3)
        .reshape(patches, heads_here, head_size)
    )
    attn_grad = jnp.transpose(unfolded, (1, 2, 0))
    return (llm_out, attn_grad)


def solution(mesh):
    return jax.shard_map(
        body,
        mesh=mesh,
        in_specs=(
            P("expert", None, "blk"),
            P("expert", None, "blk"),
            P("expert", None, "blk"),
            P("blk"),
            P("blk", None),
            P("expert", None),
            P("expert", None, None),
            P("blk", None),
            P(),
            P("blk", "expert", None),
            P("blk", "expert", None),
            P("blk", "expert", None),
            P("blk", None),
            P("blk", None),
            P("blk", None),
        ),
        out_specs=(P("blk", None), P("expert", None, "blk")),
        check_vma=False,
    )
```

profile of v0, /device:TPU:24, one launch (start us, length us, event | category | flops | bytes accessed | tf_op | source)
XLA Modules:
  0.0 795.4 jit_solution(15924565453922228203)
XLA Ops:
  7.2 0.8 reduce.12
  8.2 38.6 %all_gather.14 = bf16[1,72,4096]{2,1,0:T(8,128)(2,1)S(1)} all-gather(bf16[1,72,128]{2,1,0:T(8,128)(2,1)} %param.16), channel_id=1, replica_groups=mesh['blk'=32,'expert'=16] {'blk'}, dimensions={2}, use_global_device_ids=true | all-gather | bytes 608256 | tf_op jit(solution)/shard_map/all_gather | solution.py:51
  46.8 1.3 dynamic-slice.1
  48.7 0.8 bitcast_dynamic-update-slice_fusion
  49.5 0.8 dynamic-update-slice.1
  50.3 20.4 %all-reduce.2 = (s32[1024]{0:T(1024)S(1)}, s32[1024]{0:T(1024)S(1)}) all-reduce(s32[1024]{0:T(1024)S(1)} %bitcast_dynamic-update-slice_fusion, s32[1024]{0:T(1024)S(1)} %dynamic-update-slice.1), channel_id=2, replica_groups=mesh['blk'=32,'expert'=16] {'blk'}, use_global_device_ids=true, to_apply=%add | all-reduce | flops 2048 | bytes 16384 | tf_op jit(solution)/shard_map/all_gather | solution.py:45
  71.2 1.3 fusion.99
  72.6 38.9 %all_gather.15 = bf16[1,72,4096]{2,1,0:T(8,128)(2,1)S(1)} all-gather(bf16[1,72,128]{2,1,0:T(8,128)(2,1)S(1)} %copy-done.15), channel_id=1, replica_groups=mesh['blk'=32,'expert'=16] {'blk'}, dimensions={2}, use_global_device_ids=true | all-gather | bytes 608256 | tf_op jit(solution)/shard_map/all_gather | solution.py:52
  111.9 0.6 fusion.65
  112.9 40.9 %all-reduce.4 = (f32[32]{0:T(128)S(1)}, f32[32]{0:T(128)S(1)}) all-reduce(f32[32]{0:T(128)S(1)} %reduce_sum.118, f32[32]{0:T(128)S(1)} %reduce_sum.115), channel_id=1, replica_groups=mesh['blk'=32,'expert'=16] {'expert'}, use_global_device_ids=true, to_apply=%region_13.14 | all-reduce | flops 64 | bytes 512 | tf_op jit(solution)/shard_map/psum | solution.py:73
  154.5 1.0 convolution_convert_fusion.1
  156.1 1.0 fusion.98
  157.2 9.0 %reduce-window.14 = s32[32,8,128]{2,1,0:T(8,128)S(1)} reduce-window(s32[32,8,128]{2,1,0:T(8,128)S(1)} %fusion.62, s32[]{:T(128)} %constant.122.clone.1), window={size=1x1x128 pad=0_0x0_0x127_0}, to_apply=%region_0.1 | reduce-window | flops 4161536 | bytes 262148 | tf_op jit(solution)/shard_map/reduce-window
  166.7 18.0 %reduce-window.16 = s32[64,8,128]{2,1,0:T(8,128)S(1)} reduce-window(s32[64,8,128]{2,1,0:T(8,128)S(1)} %fusion.55, s32[]{:T(128)} %constant.122.clone.1), window={size=1x1x128 pad=0_0x0_0x127_0}, to_apply=%region_17.18 | reduce-window | flops 8323072 | bytes 524292 | tf_op jit(solution)/shard_map/reduce-window.2
  185.4 4.3 scatter_custom_fusion.3
  189.9 4.3 scatter_custom_fusion.4
  194.6 98.9 %all-reduce.9.cloned.1.call-done = bf16[32,2048]{1,0:T(8,128)(2,1)} async-done(((bf16[32,2048]{1,0:T(8,128)(2,1)}), bf16[32,2048]{1,0:T(8,128)(2,1)}) %all-reduce.9.cloned.1.call-update) | async-done | bytes 131088 | tf_op jit(solution)/shard_map/psum | solution.py:83
  293.4 1.0 broadcast_in_dim.114
  294.5 6.1 scatter_fusion
  300.6 10.1 %all-to-all-start = ((bf16[32,4,2048]{2,1,0:T(4,128)(2,1)}), bf16[32,4,2048]{2,1,0:T(4,128)(2,1)S(1)}, u32[]{:S(2)}, u32[]{:S(2)}) async-start(bf16[32,4,2048]{2,1,0:T(4,128)(2,1)} %scatter_fusion), calls=%async_computation | async-start | bytes 1048576 | tf_op jit(solution)/shard_map/all_to_all | solution.py:98
  310.7 3.1 gather_fusion.2
  313.8 4.1 gather.20
  317.9 4.3 scatter_custom_fusion.5
  322.5 4.3 scatter_custom_fusion
  326.8 4.3 scatter_custom_fusion.2
  331.3 0.9 gather_fusion
  332.7 0.8 copy-done.1
  333.7 3.0 gather_fusion.1
  336.7 2.3 gather.18
  339.0 4.0 fusion.6
  343.0 58.8 %all_to_all.30 = bf16[32,10,2048]{2,1,0:T(8,128)(2,1)} all-to-all(bf16[32,10,2048]{2,1,0:T(8,128)(2,1)S(1)} %get-tuple-element.25), channel_id=1, replica_groups=mesh['blk'=32,'expert'=16] {'blk'}, dimensions={0} | all-to-all | bytes 2621440 | tf_op jit(solution)/shard_map/all_to_all | solution.py:134
  401.8 8.2 %all-to-all-start.3 = ((bf16[32,10,2048]{2,1,0:T(8,128)(2,1)}), bf16[32,10,2048]{2,1,0:T(8,128)(2,1)}, u32[]{:S(2)}, u32[]{:S(2)}) async-start(bf16[32,10,2048]{2,1,0:T(8,128)(2,1)} %get-tuple-element.24), calls=%async_computation.3 | async-start | bytes 4194304 | tf_op jit(solution)/shard_map/all_to_all | solution.py:134
  410.0 2.6 reshape.323
  412.7 0.7 fusion.33
  413.8 0.7 fusion.37
  415.0 0.6 convolution_convert_fusion
  415.6 1.6 reshape.324
  417.2 41.7 %all-to-all-done.3 = bf16[32,10,2048]{2,1,0:T(8,128)(2,1)} async-done(((bf16[32,10,2048]{2,1,0:T(8,128)(2,1)}), bf16[32,10,2048]{2,1,0:T(8,128)(2,1)}, u32[]{:S(2)}, u32[]{:S(2)}) %all-to-all-start.3) | async-done | bytes 1310752 | tf_op jit(solution)/shard_map/all_to_all | solution.py:134
  458.9 7.6 all-to-all-start.2
  466.4 2.5 reshape.326
  469.0 1.9 fusion.29
  470.9 0.6 fusion.35
  471.5 0.5 copy-done.6
  472.0 0.6 fusion.1
  472.6 1.5 reshape.327
  474.1 39.2 %all-to-all-done.2 = bf16[32,10,2048]{2,1,0:T(8,128)(2,1)} async-done(((bf16[32,10,2048]{2,1,0:T(8,128)(2,1)}), bf16[32,10,2048]{2,1,0:T(8,128)(2,1)}, u32[]{:S(2)}, u32[]{:S(2)}) %all-to-all-start.2) | async-done | bytes 1310752 | tf_op jit(solution)/shard_map/all_to_all | solution.py:150
  513.3 9.5 %all-to-all-start.4 = ((bf16[32,10,2048]{2,1,0:T(8,128)(2,1)}), bf16[32,10,2048]{2,1,0:T(8,128)(2,1)S(1)}, u32[]{:S(2)}, u32[]{:S(2)}) async-start(bf16[32,10,2048]{2,1,0:T(8,128)(2,1)} %reshape.327), calls=%async_computation.4 | async-start | bytes 4194304 | tf_op jit(solution)/shard_map/all_to_all | solution.py:150
  522.8 3.7 reshape.329
  526.5 7.2 scatter_custom_fusion.6
  533.7 2.1 convert_element_type.139
  535.8 34.4 %all-to-all-done.4 = bf16[32,10,2048]{2,1,0:T(8,128)(2,1)S(1)} async-done(((bf16[32,10,2048]{2,1,0:T(8,128)(2,1)}), bf16[32,10,2048]{2,1,0:T(8,128)(2,1)S(1)}, u32[]{:S(2)}, u32[]{:S(2)}) %all-to-all-start.4) | async-done | bytes 1310752 | tf_op jit(solution)/shard_map/all_to_all | solution.py:150
  570.2 1.7 reshape.330
  571.9 6.2 scatter_custom_fusion.7
  578.1 0.9 convert_element_type.149
  579.0 140.3 %all-reduce.11.cloned.1.call-done = (bf16[128,2048]{1,0:T(8,128)(2,1)}, bf16[128,2048]{1,0:T(8,128)(2,1)}) async-done(((bf16[128,2048]{1,0:T(8,128)(2,1)}, bf16[128,2048]{1,0:T(8,128)(2,1)}), (bf16[128,2048]{1,0:T(8,128)(2,1)}, bf16[128,2048]{1,0:T(8,128)(2,1)})) %all-reduce.11.cloned.1.call-update) | async-done | bytes 1048592 | tf_op jit(solution)/shard_map/psum | solution.py:158
  719.3 2.3 fusion.26
  721.7 1.8 scatter_custom_fusion.8
  723.5 1.0 reshape.328
  724.5 9.8 %all-to-all-start.5 = ((bf16[32,4,2048]{2,1,0:T(4,128)(2,1)}), bf16[32,4,2048]{2,1,0:T(4,128)(2,1)S(1)}, u32[]{:S(2)}, u32[]{:S(2)}) async-start(bf16[32,4,2048]{2,1,0:T(4,128)(2,1)} %reshape.328), calls=%async_computation.5 | async-start | bytes 1048576 | tf_op jit(solution)/shard_map/all_to_all | solution.py:193
  734.5 16.0 %all-to-all-done.5 = bf16[32,4,2048]{2,1,0:T(4,128)(2,1)S(1)} async-done(((bf16[32,4,2048]{2,1,0:T(4,128)(2,1)}), bf16[32,4,2048]{2,1,0:T(4,128)(2,1)S(1)}, u32[]{:S(2)}, u32[]{:S(2)}) %all-to-all-start.5) | async-done | bytes 524320 | tf_op jit(solution)/shard_map/all_to_all | solution.py:193
  750.5 1.0 gather_fusion.3
  751.5 0.6 fusion.97
  752.1 35.1 %all-reduce.3 = (f32[32]{0:T(128)S(1)}, f32[32]{0:T(128)S(1)}) all-reduce(f32[32]{0:T(128)S(1)} %get-tuple-element.9, f32[32]{0:T(128)S(1)} %get-tuple-element.8), channel_id=1, replica_groups=mesh['blk'=32,'expert'=16] {'expert'}, use_global_device_ids=true, to_apply=%region_33.34 | all-reduce | flops 64 | bytes 512 | tf_op jit(solution)/shard_map/psum | solution.py:205
  787.4 0.7 copy.58
  (114 shorter events, 6.9 us)
Async XLA Ops:
  7.2 147.3 %copy-start = (bf16[1,288,2048]{2,1,0:T(8,128)(2,1)S(1)}, bf16[1,288,2048]{2,1,0:T(8,128)(2,1)}, u32[]{:S(2)}) copy-start(bf16[1,288,2048]{2,1,0:T(8,128)(2,1)} %param.21) | copy-start | bytes 3538948
  7.2 286.3 %all-reduce.9.cloned.1.call-start = ((), (), s32[]{:S(2)}) async-start(), calls=%async_computation.6 | async-start | bytes 262144 | tf_op jit(solution)/shard_map/psum | solution.py:83
  8.2 64.4 %copy-start.15 = (bf16[1,72,128]{2,1,0:T(8,128)(2,1)S(1)}, bf16[1,72,128]{2,1,0:T(8,128)(2,1)}, u32[]{:S(2)}) copy-start(bf16[1,72,128]{2,1,0:T(8,128)(2,1)} %param.17) | copy-start | bytes 55300
  111.9 43.7 %copy-start.16 = (s32[128,8]{0,1:T(8,128)S(1)}, s32[128,8]{0,1:T(8,128)}, u32[]{:S(2)}) copy-start(s32[128,8]{0,1:T(8,128)} %param.27) | copy-start | bytes 12292
  155.5 34.2 %copy-start.17 = (f32[128,8]{0,1:T(8,128)S(1)}, f32[128,8]{0,1:T(8,128)}, u32[]{:S(2)}) copy-start(f32[128,8]{0,1:T(8,128)} %param.28) | copy-start | bytes 12292
  155.6 38.7 %copy-start.7 = (bf16[128,2048]{1,0:T(8,128)(2,1)S(1)}, bf16[128,2048]{1,0:T(8,128)(2,1)}, u32[]{:S(2)}) copy-start(bf16[128,2048]{1,0:T(8,128)(2,1)} %param.29) | copy-start | bytes 1572868
  300.6 30.6 %all-to-all-start = ((bf16[32,4,2048]{2,1,0:T(4,128)(2,1)}), bf16[32,4,2048]{2,1,0:T(4,128)(2,1)S(1)}, u32[]{:S(2)}, u32[]{:S(2)}) async-start(bf16[32,4,2048]{2,1,0:T(4,128)(2,1)} %scatter_fusion), calls=%async_computation | async-start | bytes 1048576 | tf_op jit(solution)/shard_map/all_to_all | solution.py:98
  331.3 1.0 copy-start.13
  331.3 2.2 copy-start.14
  332.7 0.8 copy-start.1
  401.8 57.1 %all-to-all-start.3 = ((bf16[32,10,2048]{2,1,0:T(8,128)(2,1)}), bf16[32,10,2048]{2,1,0:T(8,128)(2,1)}, u32[]{:S(2)}, u32[]{:S(2)}) async-start(bf16[32,10,2048]{2,1,0:T(8,128)(2,1)} %get-tuple-element.24), calls=%async_computation.3 | async-start | bytes 4194304 | tf_op jit(solution)/shard_map/all_to_all | solution.py:134
  410.0 2.6 copy-start.5
  412.6 1.1 copy-start.3
  413.8 0.7 copy-start.10
  413.8 1.2 copy-start.12
  458.9 54.4 %all-to-all-start.2 = ((bf16[32,10,2048]{2,1,0:T(8,128)(2,1)}), bf16[32,10,2048]{2,1,0:T(8,128)(2,1)}, u32[]{:S(2)}, u32[]{:S(2)}) async-start(bf16[32,10,2048]{2,1,0:T(8,128)(2,1)} %reshape.324), calls=%async_computation.2 | async-start | bytes 4194304 | tf_op jit(solution)/shard_map/all_to_all | solution.py:150
  468.9 1.9 copy-start.4
  469.0 1.9 copy-start.11
  470.9 1.1 copy-start.6
  513.3 56.9 %all-to-all-start.4 = ((bf16[32,10,2048]{2,1,0:T(8,128)(2,1)}), bf16[32,10,2048]{2,1,0:T(8,128)(2,1)S(1)}, u32[]{:S(2)}, u32[]{:S(2)}) async-start(bf16[32,10,2048]{2,1,0:T(8,128)(2,1)} %reshape.327), calls=%async_computation.4 | async-start | bytes 4194304 | tf_op jit(solution)/shard_map/all_to_all | solution.py:150
  522.8 196.6 %all-reduce.11.cloned.1.call-start = ((), (), s32[]{:S(2)}) async-start(), calls=%async_computation.7 | async-start | bytes 2097152 | tf_op jit(solution)/shard_map/psum | solution.py:158
  578.1 141.3 %copy-start.2 = (bf16[128,2048]{1,0:T(8,128)(2,1)S(1)}, bf16[128,2048]{1,0:T(8,128)(2,1)}, u32[]{:S(2)}) copy-start(bf16[128,2048]{1,0:T(8,128)(2,1)} %copy-done.1) | copy-start | bytes 1572868
  578.1 143.6 %copy-start.8 = (bf16[128,2048]{1,0:T(8,128)(2,1)S(1)}, bf16[128,2048]{1,0:T(8,128)(2,1)}, u32[]{:S(2)}) copy-start(bf16[128,2048]{1,0:T(8,128)(2,1)} %param.29) | copy-start | bytes 1572868
  719.3 2.3 copy-start.9
  724.5 26.0 %all-to-all-start.5 = ((bf16[32,4,2048]{2,1,0:T(4,128)(2,1)}), bf16[32,4,2048]{2,1,0:T(4,128)(2,1)S(1)}, u32[]{:S(2)}, u32[]{:S(2)}) async-start(bf16[32,4,2048]{2,1,0:T(4,128)(2,1)} %reshape.328), calls=%async_computation.5 | async-start | bytes 1048576 | tf_op jit(solution)/shard_map/all_to_all | solution.py:193
Sparse Core Ops, SparseCore 0:
  155.7 137.7 all-reduce.8
  579.1 140.1 all-reduce.10
where the time goes:
time: 804 us; the launch traced here: 795 us
  waiting for transfers between devices  370 us (46%)
  blocking collectives  233 us (29%)
  local copies, waits for them, and re-layouts  67.4 us (8%)
  other arithmetic  55.3 us (7%)
  starting transfers between devices  45.3 us (6%)
  between operations  15.9 us (2%)
  matrix products  8.46 us (1%)
    psum x1, waiting for transfers between devices, to_owner(): return lax.psum(combined.astype(jnp.bfloat16), 'expert').astype(jnp.float32)  140 us
    psum x1, waiting for transfers between devices, body(): vision = lax.psum(merger_part.astype(jnp.bfloat16), 'expert')  98.9 us
    all_to_all x2, waiting for transfers between devices, to_owner(): lax.all_to_all(partial_value.astype(jnp.bfloat16).reshape(blocks, CAPX, m...  73.6 us
    all_to_all x1, blocking collectives, dispatch(): lax.all_to_all(buffer.reshape(blocks, CAPX, model_width), 'blk', split_ax...  58.8 us
    all_to_all x1, waiting for transfers between devices, dispatch(): lax.all_to_all(buffer.reshape(blocks, CAPX, model_width), 'blk', split_ax...  41.7 us
    psum x1, blocking collectives, body(): lax.psum((jnp.sum(merged, axis=1), jnp.sum(merged * merged, axis=1)), 'ex...  40.9 us
    all_gather x1, blocking collectives, body(): value_part = lax.all_gather(values, 'blk', axis=2, tiled=True)  38.9 us
    all_gather x1, blocking collectives, body(): key_part = lax.all_gather(keys, 'blk', axis=2, tiled=True)  38.6 us
  transfers between devices with their start and end apart: 7, of which 6 were waited for; matrix products, arithmetic and copies ran while one was open for 11% of the time, Pallas kernels for 0%

commit v1 on v0

v1 whole, which is shorter than its diff:
```python
import jax
import jax.numpy as jnp
from jax import lax
from jax.experimental import pallas as pl
from jax.experimental.pallas import tpu as pltpu
from jax.sharding import PartitionSpec as P

MESH = pl.DeviceIdType.MESH
F32 = jnp.float32
BF16 = jnp.bfloat16
EPS = 1e-06
NB = 32
NE = 16
NZ = 8
HD = 72
CAPX = 10
SLOT = 16
ROWS = NB * CAPX
HALF = ROWS // 2
COLS = 256
TOK = 128
MR = 32
WIDTH = 2048
FG = 192
MERGE = 4608
KVR = 160
STREAMS = ((1, 0, 4), (1, 1, 3), (-1, 0, 3), (-1, 1, 4))


def mm(a, b):
    return lax.dot_general(a, b, (((1,), (0,)), ((), ())), preferred_element_type=F32)


def mm_nt(a, b):
    return lax.dot_general(a, b, (((1,), (1,)), ((), ())), preferred_element_type=F32)


def mm_tn(a, b):
    return lax.dot_general(a, b, (((0,), (0,)), ((), ())), preferred_element_type=F32)


def iota(shape, dim):
    return lax.broadcasted_iota(jnp.int32, shape, dim)


def wait_bytes(ref, sem):
    pltpu.make_async_copy(ref, ref, sem).wait()


def kernel(
    qp_ref, kv_ref, plc_ref, rt_ref, gt_ref, gain_ref, gsp_ref, ng_ref,
    mw_hbm, text_hbm, cot_hbm, wg_hbm, wu_hbm, wd_hbm,
    llm_ref, ag_ref,
    mw, text, cot, wg, wu, wd, wgs, wus, local_sem,
    kvb, scores, kv_send, kv_recv,
    dmat, dg_hi, dg_lo, cmat, ga, gb, sa, sb,
    cot_out, cot_in, h_out, h_in, rg_out, rg_in, dn_out, dn_in, a2a_send, a2a_recv,
    cv_out, cv_in, vi_out, vi_in, hg_out, hg_in, row_send, row_recv,
    gw_all, st_all, vp, vp_all, hg_all, hg_mine, e_send, e_recv,
    vis_all, cv_all, z_send, z_recv,
    xc, xh, ring_send, ring_recv,
    gate_acc, up_acc, ss_acc, act_grad,
    rg_part, rg_o, rg_i, dn_part, dn_o, dn_i, rs_send, rs_recv,
    pair_out, pair_in, pair_send, pair_recv,
    llm_all, llm_send, llm_recv,
):
    b = lax.axis_index("blk")
    e = lax.axis_index("expert")
    y = e // NZ
    z = e % NZ
    core = b % 2
    x = (b // 2) % 4
    yh = b // 8

    def blk_of(yy, xx, cc):
        return (yy * 4 + xx) * 2 + cc

    def zdev(zz):
        return y * NZ + zz

    zcols = pl.ds(pl.multiple_of(z * COLS, COLS), COLS)
    locals_ = [
        pltpu.make_async_copy(cot_hbm.at[:, zcols], cot, local_sem.at[0]),
        pltpu.make_async_copy(text_hbm.at[:, zcols], text, local_sem.at[1]),
        pltpu.make_async_copy(mw_hbm.at[0], mw, local_sem.at[2]),
        pltpu.make_async_copy(wd_hbm.at[0], wd, local_sem.at[3]),
        pltpu.make_async_copy(wg_hbm.at[0], wg, local_sem.at[4]),
        pltpu.make_async_copy(wu_hbm.at[0], wu, local_sem.at[5]),
    ]
    for copy in locals_:
        copy.start()
    kvb[b] = kv_ref[...]

    barrier = pltpu.get_barrier_semaphore()

    def greet_blk(i, carry):
        pl.semaphore_signal(barrier, inc=1, device_id=((b + i) % NB, e), device_id_type=MESH)
        return carry

    def greet_expert(i, carry):
        pl.semaphore_signal(barrier, inc=1, device_id=(b, (e + i) % NE), device_id_type=MESH)
        return carry

    lax.fori_loop(1, NB, greet_blk, 0)
    lax.fori_loop(1, NE, greet_expert, 0)
    pl.semaphore_wait(barrier, NB - 1 + NE - 1)

    def send(src, dst, ssem, rsem, db, de):
        pltpu.make_async_remote_copy(
            src_ref=src, dst_ref=dst, send_sem=ssem, recv_sem=rsem, device_id=(db, de), device_id_type=MESH
        ).start()

    def a2a_start(src, dst, ssem, rsem):
        dst[b] = src[b]

        def one(i, carry):
            to = (b + i) % NB
            send(src.at[to], dst.at[b], ssem, rsem, to, e)
            return carry

        lax.fori_loop(1, NB, one, 0)

    def a2a_wait(dst, rsem):
        wait_bytes(dst.at[pl.ds(0, NB - 1)], rsem)

    def to_experts(src_of, dst, ssem, rsem):
        def one(i, carry):
            to = (e + i) % NE
            send(src_of(to), dst.at[e], ssem, rsem, b, to)
            return carry

        lax.fori_loop(1, NE, one, 0)

    def to_z(src, dst, ssem, rsem):
        def one(i, carry):
            to = (z + i) % NZ
            send(src, dst.at[z], ssem, rsem, b, zdev(to))
            return carry

        lax.fori_loop(1, NZ, one, 0)

    def ring_gather(buf, ssem, rsems, half_rows):
        def piece(src, half):
            return buf.at[src, pl.ds(half * half_rows, half_rows)]

        for k in range(5):
            for way, half, far in STREAMS:
                if k > far:
                    continue
                src = (z + 8 - way * k) % NZ
                if k > 0:
                    wait_bytes(piece(src, half), rsems.at[src * 2 + half])
                if k < far:
                    send(piece(src, half), piece(src, half), ssem, rsems.at[src * 2 + half], b, zdev((z + 8 + way) % NZ))
            yield k

    def ring_reduce(part, out, inn, ssem, rsems):
        for d in range(4, 0, -1):
            for index, (way, half, far) in enumerate(STREAMS):
                if d > far:
                    continue
                rows = pl.ds(half * HALF, HALF)
                dest = (z + 8 + way * d) % NZ
                value = part[dest, rows, :]
                here = index * 5 + d
                if d < far:
                    wait_bytes(inn.at[here], rsems.at[here])
                    value = value + inn[here].astype(F32)
                out[here] = value.astype(BF16)
                send(out.at[here], inn.at[here - 1], ssem, rsems.at[here - 1], b, zdev((z + 8 + way) % NZ))
            yield d
        for index in range(4):
            wait_bytes(inn.at[index * 5], rsems.at[index * 5])
        for half in range(2):
            rows = pl.ds(half * HALF, HALF)
            part[z, rows, :] = part[z, rows, :] + (inn[half * 5].astype(F32) + inn[(2 + half) * 5].astype(F32))
        yield 0

    def kv_go(block, to):
        send(kvb.at[block], kvb.at[block], kv_send.at[0], kv_recv.at[block], to, e)

    def kv_x(block):
        for dx in (1, 3, 2):
            kv_go(block, blk_of(yh, (x + dx) % 4, core))
        kv_go(block, blk_of(yh, x, 1 - core))

    for dy in (1, 3, 2):
        kv_go(b, blk_of((yh + dy) % 4, x, core))
    kv_x(b)

    upper = (iota((TOK, TOK), 0) < iota((TOK, TOK), 1)).astype(BF16)
    ids = 2 * iota((NB, TOK), 0) + y
    hit = jnp.zeros((NB, TOK), F32)
    gate = jnp.zeros((NB, TOK), F32)
    for k in range(8):
        same = rt_ref[k : k + 1, :] == ids
        hit = hit + jnp.where(same, 1.0, 0.0)
        gate = gate + jnp.where(same, gt_ref[k : k + 1, :], 0.0)
    rank = mm(hit.astype(BF16), upper)
    place = jnp.where(hit > 0.0, rank, -1.0)
    slot3 = iota((NB, SLOT, TOK), 1).astype(F32)
    one_hot = jnp.where(place[:, None, :] == slot3, 1.0, 0.0)
    gated = (one_hot * gate[:, None, :]).reshape(NB * SLOT, TOK)
    dmat[...] = one_hot.reshape(NB * SLOT, TOK).astype(BF16)
    high = gated.astype(BF16)
    dg_hi[...] = high
    dg_lo[...] = (gated - high.astype(F32)).astype(BF16)
    slot_gate = jnp.sum(gated, axis=1, keepdims=True)
    locals_[0].wait()
    back = (mm(dmat[...], cot[...]) * slot_gate).astype(BF16)
    cot_out[...] = back.reshape(NB, SLOT, COLS)

    for dy in (1, 3, 2):
        block = blk_of((yh + 4 - dy) % 4, x, core)
        wait_bytes(kvb.at[block], kv_recv.at[block])
        kv_x(block)
    a2a_start(cot_out, cot_in, a2a_send.at[0], a2a_recv.at[0])

    ci = iota((ROWS, NB * SLOT), 0)
    cj = iota((ROWS, NB * SLOT), 1)
    cmat[...] = jnp.where((ci == (cj >> 4) * CAPX + (cj & 15)) & ((cj & 15) < CAPX), 1.0, 0.0).astype(BF16)

    def kv_arrived_x(i, carry):
        dx = jnp.where(i < 4, 1, jnp.where(i < 8, 3, 2))
        block = blk_of((yh + 4 - i % 4) % 4, (x + 4 - dx) % 4, core)
        wait_bytes(kvb.at[block], kv_recv.at[block])
        kv_go(block, blk_of(yh, x, 1 - core))
        return carry

    lax.fori_loop(0, 12, kv_arrived_x, 0)

    locals_[2].wait()
    gw = mm(gsp_ref[...], mw[...])
    gw = gw[0:1, :] + gw[1:2, :]
    for c in range(NZ):
        gw_all[e, c : c + 1, :] = gw[:, c * COLS : (c + 1) * COLS]
    to_experts(lambda to: gw_all.at[e], gw_all, e_send.at[0], e_recv.at[0])

    def kv_arrived_core(i, carry):
        block = 2 * i + (1 - core)
        wait_bytes(kvb.at[block], kv_recv.at[block])
        return carry

    lax.fori_loop(0, 16, kv_arrived_core, 0)

    def score_block(i, carry):
        s = mm_tn(kvb[i], qp_ref[...])
        scores[pl.ds(pl.multiple_of(i * TOK, TOK), TOK), :] = s
        return jnp.maximum(carry, jnp.max(s.reshape(TOK // 8, 8, TOK), axis=0))

    top = lax.fori_loop(0, NB, score_block, jnp.full((8, TOK), -3e38, F32))
    top = jnp.max(top, axis=0, keepdims=True)

    def weigh_block(i, carry):
        acc, total = carry
        s = scores[pl.ds(pl.multiple_of(i * TOK, TOK), TOK), :]
        w = jnp.exp((s - top) * (HD ** -0.5))
        acc = acc + mm(kvb[i], w.astype(BF16))
        return acc, total + jnp.sum(w.reshape(TOK // 8, 8, TOK), axis=0)

    acc, total = lax.fori_loop(0, NB, weigh_block, (jnp.zeros((KVR, TOK), F32), jnp.zeros((8, TOK), F32)))
    total = jnp.sum(total, axis=0, keepdims=True)
    attn = (acc[HD : 2 * HD, :] / total).astype(BF16).astype(F32)

    def over_i(row):
        row = row + pltpu.roll(row, 32, 1)
        return row + pltpu.roll(row, 64, 1)

    sums = jnp.sum(attn, axis=0, keepdims=True)
    squares = jnp.sum(attn * attn, axis=0, keepdims=True)
    row8 = iota((8, TOK), 0)
    st_all[e] = over_i(jnp.where(row8 == 0, sums, jnp.where(row8 == 1, squares, 0.0)))
    to_experts(lambda to: st_all.at[e], st_all, e_send.at[1], e_recv.at[1])

    a2a_wait(cot_in, a2a_recv.at[0])
    xc[z] = mm(cmat[...], cot_in[...].reshape(NB * SLOT, COLS)).astype(BF16)
    cot_ring = ring_gather(xc, ring_send.at[0], ring_recv.at[0], HALF)
    next(cot_ring)

    wait_bytes(st_all.at[pl.ds(0, NE - 1)], e_recv.at[1])
    stats = jnp.sum(st_all[...], axis=0)
    mean = stats[0:1, :] * (1.0 / MERGE)
    inv_std = lax.rsqrt(stats[1:2, :] * (1.0 / MERGE) - mean * mean + EPS)
    normed = (attn - mean) * inv_std
    scaled = normed * gain_ref[...]
    group = iota((HD, TOK), 1) >> 5
    left = jnp.concatenate([jnp.where(group == i, scaled, 0.0) for i in range(4)], axis=0).astype(BF16)

    def merge_chunk(c, carry):
        cols = pl.ds(pl.multiple_of(c * COLS, COLS), COLS)
        v = mm_tn(left, mw[:, cols])
        vp[c] = (v[0:32] + v[32:64] + v[64:96] + v[96:128]).astype(BF16)
        return carry

    lax.fori_loop(0, NZ, merge_chunk, 0)
    vp_all[e] = vp[z]
    to_experts(lambda to: vp.at[to % NZ], vp_all, e_send.at[2], e_recv.at[2])

    places = kvb[:, 144:160, :].astype(F32)
    places = jnp.sum(jnp.where(iota((NB, 16, TOK), 1) == 3, places, 0.0), axis=1)
    named = jnp.where(places == b.astype(F32), 1.0, 0.0)
    count = jnp.broadcast_to(jnp.sum(named, axis=1, keepdims=True), (NB, TOK))
    below = (iota((NB, NB), 1) < iota((NB, NB), 0)).astype(BF16)
    base = mm(below, count.astype(BF16))
    placed = jnp.sum(count, axis=0, keepdims=True)[:, 0:1]
    q3 = iota((NB, 8, TOK), 1).astype(F32)
    k3 = jnp.where(q3 < 4.0, q3, q3 - 4.0)
    lane3 = iota((NB, 8, TOK), 2).astype(F32)
    mine = jnp.where((lane3 == base[:, None, :] + k3) & (k3 < count[:, None, :]), 1.0, 0.0)
    ga[...] = jnp.where(q3 < 4.0, mine, 0.0).reshape(NB * 8, TOK).astype(BF16)
    gb[...] = jnp.where(q3 < 4.0, 0.0, mine).reshape(NB * 8, TOK).astype(BF16)
    to_shard = jnp.where(plc_ref[0:1, :] == iota((NB, TOK), 0), 1.0, 0.0)
    order = mm(to_shard.astype(BF16), upper)
    order = jnp.where(to_shard > 0.0, order, -1.0)
    theirs = jnp.where(order[:, None, :] == k3, 1.0, 0.0)
    sa[...] = jnp.where(q3 < 4.0, theirs, 0.0).reshape(NB * 8, TOK).astype(BF16)
    sb[...] = jnp.where(q3 < 4.0, 0.0, theirs).reshape(NB * 8, TOK).astype(BF16)

    cv_out[...] = (mm(ga[...], cot[:, 0:TOK]) + mm(gb[...], cot[:, TOK:COLS])).reshape(NB, 8, TOK)
    a2a_start(cv_out, cv_in, row_send.at[0], row_recv.at[0])
    next(cot_ring)

    wait_bytes(vp_all.at[pl.ds(0, NE - 1)], e_recv.at[2])
    vision = jnp.sum(vp_all[...].astype(F32), axis=0).astype(BF16)
    vis_all[z] = vision
    fill = jnp.zeros((TOK - MR, COLS), BF16)
    padded = jnp.concatenate([vision, fill], axis=0)
    vi_out[...] = (mm(sa[...], padded[:, 0:TOK]) + mm(sb[...], padded[:, TOK:COLS])).reshape(NB, 8, TOK)
    a2a_start(vi_out, vi_in, row_send.at[1], row_recv.at[1])
    to_z(vis_all.at[z], vis_all, z_send.at[0], z_recv.at[0])
    next(cot_ring)

    locals_[4].wait()
    locals_[5].wait()

    def gain_chunk(c, carry):
        cols = pl.ds(pl.multiple_of(c * COLS, COLS), COLS)
        g = ng_ref[:, cols]
        wgs[:, cols] = (wg[:, cols].astype(F32) * g).astype(BF16)
        wus[:, cols] = (wu[:, cols].astype(F32) * g).astype(BF16)
        return carry

    lax.fori_loop(0, NZ, gain_chunk, 0)
    a2a_wait(cv_in, row_recv.at[0])
    cv = cv_in[...].reshape(NB * 8, TOK).astype(BF16)
    cv_all[z, :, 0:TOK] = mm_tn(sa[...], cv)[0:MR].astype(BF16)
    cv_all[z, :, TOK:COLS] = mm_tn(sb[...], cv)[0:MR].astype(BF16)
    to_z(cv_all.at[z], cv_all, z_send.at[1], z_recv.at[1])

    locals_[1].wait()
    a2a_wait(vi_in, row_recv.at[1])
    arrived = vi_in[...].reshape(NB * 8, TOK).astype(BF16)
    taken = iota((TOK, TOK), 0).astype(F32) < placed
    llm_a = jnp.where(taken, mm_tn(ga[...], arrived), text[:, 0:TOK].astype(F32))
    llm_b = jnp.where(taken, mm_tn(gb[...], arrived), text[:, TOK:COLS].astype(F32))
    text[:, 0:TOK] = llm_a.astype(BF16)
    text[:, TOK:COLS] = llm_b.astype(BF16)
    h_out[...] = mm(dmat[...], text[...]).astype(BF16).reshape(NB, SLOT, COLS)
    a2a_start(h_out, h_in, a2a_send.at[1], a2a_recv.at[1])

    for _ in cot_ring:
        pass
    locals_[3].wait()
    act_grad[...] = jnp.zeros_like(act_grad)
    gate_acc[...] = jnp.zeros_like(gate_acc)
    up_acc[...] = jnp.zeros_like(up_acc)
    ss_acc[...] = jnp.zeros_like(ss_acc)

    def act_chunk(c, carry):
        cols = pl.ds(pl.multiple_of(c * COLS, COLS), COLS)
        act_grad[...] += mm_nt(xc[c], wd[:, cols])
        return carry

    lax.fori_loop(0, NZ, act_chunk, 0)

    a2a_wait(h_in, a2a_recv.at[1])
    xh[z] = mm(cmat[...], h_in[...].reshape(NB * SLOT, COLS)).astype(BF16)
    h_ring = ring_gather(xh, ring_send.at[1], ring_recv.at[1], HALF)

    def project(c, carry):
        cols = pl.ds(pl.multiple_of(c * COLS, COLS), COLS)
        rows = xh[c]
        gate_acc[...] += mm_nt(rows, wgs[:, cols])
        up_acc[...] += mm_nt(rows, wus[:, cols])
        wide = rows.astype(F32)
        ss_acc[...] += wide[:, 0:TOK] * wide[:, 0:TOK] + wide[:, TOK:COLS] * wide[:, TOK:COLS]
        return carry

    for k in h_ring:
        if k == 0 or k == 4:
            project((z + k) % NZ, 0)
        else:
            lax.fori_loop(0, 2, lambda j, carry: project((z + 8 + (2 * j - 1) * k) % NZ, carry), 0)

    inv = lax.rsqrt(jnp.sum(ss_acc[...], axis=1, keepdims=True) * (1.0 / WIDTH) + EPS)
    gate_pre = gate_acc[...] * inv
    up_proj = up_acc[...] * inv
    sig = 1.0 / (1.0 + jnp.exp(-gate_pre))
    activated = (gate_pre * sig * up_proj).astype(BF16)
    grad = act_grad[...]
    gate_grad = (grad * up_proj * sig * (1.0 + gate_pre * (1.0 - sig))).astype(BF16)
    up_grad = (grad * gate_pre * sig).astype(BF16)

    def grad_chunk(c, carry):
        cols = pl.ds(pl.multiple_of(c * COLS, COLS), COLS)
        rg_part[c] = mm(gate_grad, wg[:, cols]) + mm(up_grad, wu[:, cols])
        return carry

    def down_chunk(c, carry):
        cols = pl.ds(pl.multiple_of(c * COLS, COLS), COLS)
        dn_part[c] = mm(activated, wd[:, cols])
        return carry

    lax.fori_loop(0, NZ, grad_chunk, 0)
    rg_ring = ring_reduce(rg_part, rg_o, rg_i, rs_send.at[0], rs_recv.at[0])
    next(rg_ring)
    lax.fori_loop(0, NZ, down_chunk, 0)
    dn_ring = ring_reduce(dn_part, dn_o, dn_i, rs_send.at[1], rs_recv.at[1])
    next(rg_ring)
    next(rg_ring)
    next(dn_ring)
    next(rg_ring)
    next(rg_ring)

    def give_back(part, out, inn, index):
        out[...] = mm_tn(cmat[...], part[z].astype(BF16)).astype(BF16).reshape(NB, SLOT, COLS)
        a2a_start(out, inn, a2a_send.at[index], a2a_recv.at[index])

    give_back(rg_part, rg_out, rg_in, 2)
    next(dn_ring)

    a2a_wait(rg_in, a2a_recv.at[2])
    hidden = mm_tn(dmat[...], rg_in[...].reshape(NB * SLOT, COLS)).astype(BF16)
    hg_out[...] = (mm(ga[...], hidden[:, 0:TOK]) + mm(gb[...], hidden[:, TOK:COLS])).reshape(NB, 8, TOK)
    a2a_start(hg_out, hg_in, row_send.at[2], row_recv.at[2])
    next(dn_ring)
    next(dn_ring)
    next(dn_ring)
    give_back(dn_part, dn_out, dn_in, 3)

    a2a_wait(hg_in, row_recv.at[2])
    hg = hg_in[...].reshape(NB * 8, TOK).astype(BF16)
    hg_mine[:, 0:TOK] = mm_tn(sa[...], hg)[0:MR].astype(BF16)
    hg_mine[:, TOK:COLS] = mm_tn(sb[...], hg)[0:MR].astype(BF16)
    hg_all[e] = hg_mine[...]
    to_experts(lambda to: hg_mine, hg_all, e_send.at[3], e_recv.at[3])

    a2a_wait(dn_in, a2a_recv.at[3])
    dn = dn_in[...].reshape(NB * SLOT, COLS)
    mine_sum = mm_tn(dg_hi[...], dn) + mm_tn(dg_lo[...], dn)
    pair_out[...] = mine_sum.astype(BF16)
    send(pair_out, pair_in, pair_send.at[0], pair_recv.at[0], b, (1 - y) * NZ + z)

    wait_bytes(vis_all.at[pl.ds(0, NZ - 1)], z_recv.at[0])
    wait_bytes(cv_all.at[pl.ds(0, NZ - 1)], z_recv.at[1])
    wait_bytes(gw_all.at[pl.ds(0, NE - 1)], e_recv.at[0])
    wait_bytes(hg_all.at[pl.ds(0, NE - 1)], e_recv.at[3])
    wait_bytes(pair_in, pair_recv.at[0])
    layer = pair_out[...].astype(F32) + pair_in[...].astype(F32)
    llm_all[z] = (text[...].astype(F32) + layer).astype(BF16)
    llm_ring = ring_gather(llm_all, llm_send.at[0], llm_recv.at[0], TOK // 2)
    next(llm_ring)

    gw_sum = jnp.sum(gw_all[...], axis=0)
    ssq = jnp.zeros((MR, COLS), F32)
    cross = jnp.zeros((MR, COLS), F32)
    for c in range(NZ):
        v = vis_all[c].astype(F32)
        ghg = (hg_all[c].astype(F32) + hg_all[NZ + c].astype(F32)) * ng_ref[:, c * COLS : (c + 1) * COLS]
        ssq = ssq + v * v
        cross = cross + ghg * v
    r = lax.rsqrt(jnp.sum(ssq, axis=1, keepdims=True) * (1.0 / WIDTH) + EPS)
    pull = jnp.sum(cross, axis=1, keepdims=True) * (1.0 / WIDTH) * r * r * r
    dot_g = jnp.zeros((MR, COLS), F32)
    dot_v = jnp.zeros((MR, COLS), F32)
    back_scaled = jnp.zeros((4 * HD, TOK), F32)
    for c in range(NZ):
        v = vis_all[c].astype(F32)
        ghg = (hg_all[c].astype(F32) + hg_all[NZ + c].astype(F32)) * ng_ref[:, c * COLS : (c + 1) * COLS]
        vg = (cv_all[c].astype(F32) + (r * ghg - v * pull)).astype(BF16)
        wide = vg.astype(F32)
        dot_g = dot_g + wide * gw_sum[c : c + 1, :]
        dot_v = dot_v + wide * v
        four = jnp.concatenate([vg, vg, vg, vg], axis=0)
        back_scaled = back_scaled + mm_nt(mw[:, c * COLS : (c + 1) * COLS], four)
    next(llm_ring)

    def to_lanes(columns):
        column = jnp.sum(columns, axis=1, keepdims=True)
        column = jnp.concatenate([column, column, column, column], axis=0)
        eye = iota((TOK, TOK), 0) == iota((TOK, TOK), 1)
        return jnp.sum(jnp.where(eye, column, 0.0), axis=0, keepdims=True)

    grad_mean = to_lanes(dot_g) * (1.0 / MERGE)
    cross_mean = to_lanes(dot_v) * (1.0 / MERGE)
    scaled_grad = jnp.zeros((HD, TOK), F32)
    for i in range(4):
        scaled_grad = jnp.where(group == i, back_scaled[i * HD : (i + 1) * HD, :], scaled_grad)
    merged_grad = inv_std * (scaled_grad * gain_ref[...] - grad_mean - normed * cross_mean)
    li = iota((TOK, TOK), 0)
    unfold = jnp.where(iota((TOK, TOK), 1) == 4 * (li & 31) + (li >> 5), 1.0, 0.0).astype(BF16)
    part1 = merged_grad.astype(BF16)
    rest = merged_grad - part1.astype(F32)
    part2 = rest.astype(BF16)
    part3 = (rest - part2.astype(F32)).astype(BF16)
    ag_ref[...] = mm(part1, unfold) + mm(part2, unfold) + mm(part3, unfold)
    for _ in llm_ring:
        pass
    for c in range(NZ):
        llm_ref[:, c * COLS : (c + 1) * COLS] = llm_all[c]

    wait_bytes(kvb.at[pl.ds(0, NB - 1)], kv_send.at[0])
    for index, buf in enumerate((cot_out, h_out, rg_out, dn_out)):
        wait_bytes(buf.at[pl.ds(0, NB - 1)], a2a_send.at[index])
    for index, buf in enumerate((cv_out, vi_out, hg_out)):
        wait_bytes(buf.at[pl.ds(0, NB - 1)], row_send.at[index])
    for index, buf in enumerate((gw_all, st_all, vp_all, hg_all)):
        wait_bytes(buf.at[pl.ds(0, NE - 1)], e_send.at[index])
    for index, buf in enumerate((vis_all, cv_all)):
        wait_bytes(buf.at[pl.ds(0, NZ - 1)], z_send.at[index])
    for index, buf in enumerate((xc, xh)):
        wait_bytes(buf.at[pl.ds(0, NZ - 1)], ring_send.at[index])
    for index, buf in enumerate((rg_o, dn_o)):
        wait_bytes(buf.at[pl.ds(0, 14)], rs_send.at[index])
    wait_bytes(pair_out, pair_send.at[0])
    wait_bytes(llm_all.at[pl.ds(0, NZ - 1)], llm_send.at[0])


def scratch_shapes():
    V = pltpu.VMEM
    D = pltpu.SemaphoreType.DMA
    routed = [V((NB, SLOT, COLS), BF16)] * 8
    rows = [V((NB, 8, TOK), F32)] * 6
    reduce_bufs = [V((NZ, ROWS, COLS), F32), V((20, HALF, COLS), BF16), V((20, HALF, COLS), BF16)]
    return (
        [V((4 * HD, WIDTH), BF16), V((TOK, COLS), BF16), V((TOK, COLS), BF16)]
        + [V((FG, WIDTH), BF16)] * 5
        + [D((6,))]
        + [V((NB, KVR, TOK), BF16), V((NB * TOK, TOK), F32), D((1,)), D((NB,))]
        + [V((NB * SLOT, TOK), BF16)] * 3
        + [V((ROWS, NB * SLOT), BF16)]
        + [V((NB * 8, TOK), BF16)] * 4
        + routed + [D((4,)), D((4,))]
        + rows + [D((3,)), D((3,))]
        + [V((NE, NZ, COLS), F32), V((NE, 8, TOK), F32), V((NZ, MR, COLS), BF16), V((NE, MR, COLS), BF16)]
        + [V((NE, MR, COLS), BF16), V((MR, COLS), BF16), D((4,)), D((4,))]
        + [V((NZ, MR, COLS), BF16)] * 2 + [D((2,)), D((2,))]
        + [V((NZ, ROWS, COLS), BF16)] * 2 + [D((2,)), D((2, 16))]
        + [V((ROWS, FG), F32), V((ROWS, FG), F32), V((ROWS, TOK), F32), V((ROWS, FG), F32)]
        + reduce_bufs + reduce_bufs + [D((2,)), D((2, 20))]
        + [V((TOK, COLS), BF16)] * 2 + [D((1,)), D((1,))]
        + [V((NZ, TOK, COLS), BF16), D((1,)), D((1, 16))]
    )


def body(
    queries, keys, values, image_ids, placement, merge_gain, merge_weight, text, norm_gain,
    w_gate, w_up, w_down, routes, route_gates, cotangent,
):
    three = jnp.arange(3, dtype=jnp.int32)[:, None]
    dest = placement[:, 0]
    key_ids = (jnp.repeat(image_ids, 4)[None, :] == three).astype(BF16)
    place_row = jnp.pad(dest, (0, TOK - MR), constant_values=-1)[None, :]
    kv = jnp.concatenate(
        [keys[0], values[0], key_ids, place_row.astype(BF16), jnp.zeros((12, TOK), BF16)], axis=0
    )
    queries = queries[0].reshape(HD, MR, 4).transpose(0, 2, 1).reshape(HD, TOK)
    other = jnp.where(jnp.tile(image_ids, 4)[None, :] == three, 0.0, -1e30).astype(BF16)
    qp = jnp.concatenate([queries, jnp.zeros((HD, TOK), BF16), other, jnp.zeros((13, TOK), BF16)], axis=0)
    plc = jnp.broadcast_to(place_row, (8, TOK))
    gain = jnp.repeat(merge_gain.reshape(4, HD).T, MR, axis=1)
    gain_hi = merge_gain.astype(BF16)
    gain_lo = (merge_gain - gain_hi.astype(F32)).astype(BF16)
    gsp = jnp.concatenate([gain_hi, gain_lo, jnp.zeros((14, 4 * HD), BF16)], axis=0)
    vm = pl.BlockSpec(memory_space=pltpu.VMEM)
    anywhere = pl.BlockSpec(memory_space=pl.ANY)
    llm_out, attn_grad = pl.pallas_call(
        kernel,
        out_shape=(
            jax.ShapeDtypeStruct((TOK, WIDTH), BF16),
            jax.ShapeDtypeStruct((HD, TOK), F32),
        ),
        in_specs=[vm] * 8 + [anywhere] * 6,
        out_specs=(vm, vm),
        scratch_shapes=scratch_shapes(),
        compiler_params=pltpu.CompilerParams(
            collective_id=0, has_side_effects=True, vmem_limit_bytes=50 * 1024 * 1024
        ),
    )(
        qp, kv, plc, routes.T, route_gates.T, gain, gsp, norm_gain[None, :],
        merge_weight, text, cotangent, w_gate, w_up, w_down,
    )
    return llm_out, attn_grad[None]


def solution(mesh):
    return jax.shard_map(
        body,
        mesh=mesh,
        in_specs=(
            P("expert", None, "blk"),
            P("expert", None, "blk"),
            P("expert", None, "blk"),
            P("blk"),
            P("blk", None),
            P("expert", None),
            P("expert", None, None),
            P("blk", None),
            P(),
            P("blk", "expert", None),
            P("blk", "expert", None),
            P("blk", "expert", None),
            P("blk", None),
            P("blk", None),
            P("blk", None),
        ),
        out_specs=(P("blk", None), P("expert", None, "blk")),
        check_vma=False,
    )
```

time: 804 us -> 183 us (0.23)
  the two profiles are of different devices: /device:TPU:24 before, /device:TPU:8 now
where the time goes in v1:
time: 183 us; the launch traced here: 182 us
  Pallas kernels  166 us (91%)
  local copies, waits for them, and re-layouts  13.5 us (7%)
    pallas_call x1, Pallas kernels, body(): pl.pallas_call(kernel, out_shape=(jax.ShapeDtypeStruct((TOK, WIDTH), BF16...  166 us
    unnamed x19, local copies, waits for them, and re-layouts  9.8 us

profile of v1, /device:TPU:8, one launch (start us, length us, event | category | flops | bytes accessed | tf_op | source)
XLA Modules:
  0.0 181.9 jit_solution(12095688891820412817)
XLA Ops:
  0.6 0.1 pad.7.clone
  0.7 0.1 pad.11.clone
  0.8 0.1 pad.9.clone
  0.9 0.7 fusion.2
  1.5 0.7 tile.2
  2.2 0.1 eq.30
  2.3 0.8 fusion.1
  3.1 0.1 reshape.19
  3.2 0.1 maximum_maximum_fusion.1.gsp_ref
  3.2 0.7 broadcast_in_dim.43
  4.0 0.1 eq.34
  4.1 0.8 copy.19
  4.9 0.1 copy.21
  5.0 0.1 maximum_maximum_fusion.qp_ref
  5.2 1.6 concatenate.10.kv_ref
  6.8 0.1 copy.22.gain_ref
  6.9 0.0 copy-start
  6.9 1.1 copy-done
  8.0 0.0 copy-start.1
  8.0 1.1 copy-done.1
  9.1 0.0 copy-start.2
  9.1 1.1 copy-done.2
  10.3 0.0 copy-start.3
  10.3 1.0 copy-done.3
  11.3 0.0 copy-start.4
  11.3 1.0 copy-done.4
  12.4 0.0 copy-start.5
  12.4 0.7 copy-done.5
  13.1 0.0 copy-start.6
  13.1 0.7 copy-done.6
  13.7 0.0 copy-start.7
  13.7 0.7 copy-done.7
  14.4 166.0 %shard_map.158 = (bf16[128,2048]{1,0:T(8,128)(2,1)S(1)}, f32[72,128]{1,0:T(8,128)S(1)}) custom-call(bf16[160,128]{1,0:T(8,128)(2,1)S(1)} %maximum_maximum_fusion.qp_ref, bf16[160,128]{1,0:T(8,128)(2,1)S(1)} %concatenate.10.kv_ref, s32[8,128]{1,0:T(8,128)S(1)} %broadcast_in_dim.45.plc_ref, s32[8,128]{1,0:T(8,128)S(1)} %bitcast.17, f32[8,128]{1,0:T(8,128)S(1)} %bitcast.18, ...), custom_call_target="tpu_custom_call" | custom-call | tf_op jit(solution)/shard_map/pallas_call | solution.py:577
  180.5 0.8 copy.25
  181.3 0.6 copy.26
  (9 shorter events, 0.0 us)
Async XLA Ops:
  6.9 1.1 copy-start
  8.0 1.1 copy-start.1
  9.1 1.1 copy-start.2
  10.3 1.0 copy-start.3
  11.3 1.0 copy-start.4
  12.4 0.7 copy-start.5
  13.1 0.7 copy-start.6
  13.7 0.7 copy-start.7

commit v2 on v1

v2 whole, which is shorter than its diff:
```python
import jax
import jax.numpy as jnp
from jax import lax
from jax.experimental import pallas as pl
from jax.experimental.pallas import tpu as pltpu
from jax.sharding import PartitionSpec as P

MESH = pl.DeviceIdType.MESH
F32 = jnp.float32
BF16 = jnp.bfloat16
EPS = 1e-06
NB = 32
NE = 16
NZ = 8
HD = 72
CAPX = 10
SLOT = 16
ROWS = NB * CAPX
HALF = ROWS // 2
QUARTER = HALF // 2
SET = NB // 2
COLS = 256
TOK = 128
MR = 32
WIDTH = 2048
FG = 192
MERGE = 4608
VMEM_BYTES = 63 * 1024 * 1024
KVR = 160
STREAMS = ((1, 0, 4), (1, 1, 3), (-1, 0, 3), (-1, 1, 4))


def mm(a, b):
    return lax.dot_general(a, b, (((1,), (0,)), ((), ())), preferred_element_type=F32)


def mm_nt(a, b):
    return lax.dot_general(a, b, (((1,), (1,)), ((), ())), preferred_element_type=F32)


def mm_tn(a, b):
    return lax.dot_general(a, b, (((0,), (0,)), ((), ())), preferred_element_type=F32)


def iota(shape, dim):
    return lax.broadcasted_iota(jnp.int32, shape, dim)


def wait_bytes(ref, sem):
    pltpu.make_async_copy(ref, ref, sem).wait()


def kernel(
    q_hbm, k_hbm, v_hbm, ids_hbm, place_hbm, gain_hbm, mw_hbm, text_hbm, ng_hbm,
    wg_hbm, wu_hbm, wd_hbm, routes_hbm, gates_hbm, cot_hbm,
    llm_ref, ag_ref,
    q_in, k_in, v_in, ids_in, place_in, gain_in, ng_ref, routes_in, gates_in,
    mw, text, cot, wg, wu, wd, wgs, wus, local_sem,
    kvb, kv_send, kv_recv,
    dmat, dg_hi, dg_lo, cmat, ga, gb, sa, sb,
    cot_out, cot_in, h_out, h_in, rg_out, rg_in, dn_out, dn_in, a2a_send, a2a_recv, set_recv,
    cv_out, cv_in, vi_out, vi_in, hg_out, hg_in, row_send, row_recv,
    gw_all, st_all, vp, vp_all, hg_all, hg_mine, e_send, e_recv,
    vis_all, cv_all, z_send, z_recv,
    xc, xh, ring_send, ring_recv,
    gate_acc, up_acc, ss_acc, act_grad, hidden,
    rs_out, rs_in, rs_send, rs_recv,
    pair_out, pair_in, pair_send, pair_recv,
    llm_all, llm_send, llm_recv,
):
    b = lax.axis_index("blk")
    e = lax.axis_index("expert")
    y = e // NZ
    z = e % NZ
    core = b % 2
    x = (b // 2) % 4
    yh = b // 8

    def blk_of(yy, xx, cc):
        return (yy * 4 + xx) * 2 + cc

    def zdev(zz):
        return y * NZ + zz

    zcols = pl.ds(pl.multiple_of(z * COLS, COLS), COLS)
    pairs = (
        (k_hbm.at[0], k_in), (v_hbm.at[0], v_in), (ids_hbm, ids_in), (place_hbm, place_in), (q_hbm.at[0], q_in),
        (routes_hbm, routes_in), (gates_hbm, gates_in), (gain_hbm, gain_in), (ng_hbm, ng_ref),
        (cot_hbm.at[:, zcols], cot), (mw_hbm.at[0], mw), (text_hbm.at[:, zcols], text),
        (wg_hbm.at[0], wg), (wu_hbm.at[0], wu), (wd_hbm.at[0], wd),
    )
    locals_ = [pltpu.make_async_copy(src, dst, local_sem.at[i]) for i, (src, dst) in enumerate(pairs)]
    for copy in locals_:
        copy.start()

    barrier = pltpu.get_barrier_semaphore()

    def greet_blk(i, carry):
        pl.semaphore_signal(barrier, inc=1, device_id=((b + i) % NB, e), device_id_type=MESH)
        return carry

    def greet_expert(i, carry):
        pl.semaphore_signal(barrier, inc=1, device_id=(b, (e + i) % NE), device_id_type=MESH)
        return carry

    lax.fori_loop(1, NB, greet_blk, 0)
    lax.fori_loop(1, NE, greet_expert, 0)

    for copy in locals_[:4]:
        copy.wait()
    ids16 = jnp.broadcast_to(ids_in[...], (16, MR)).astype(F32).astype(BF16)
    ri = iota((MR, TOK), 0)
    li = iota((MR, TOK), 1)
    row16 = iota((16, TOK), 0)
    patch_ids = mm(ids16, jnp.where(li >> 2 == ri, 1.0, 0.0).astype(BF16))
    place16 = jnp.broadcast_to(place_in[...], (16, MR)).astype(F32).astype(BF16)
    place_row = mm(place16, jnp.where(li == ri, 1.0, 0.0).astype(BF16))[0:1, :]
    place_row = jnp.where(iota((1, TOK), 1) < MR, place_row, -1.0)
    extra = jnp.where(row16 < 3, jnp.where(patch_ids == row16.astype(F32), 1.0, 0.0), 0.0)
    extra = jnp.where(row16 == 3, place_row, extra)
    kvb[b] = jnp.concatenate([k_in[...].astype(F32), v_in[...].astype(F32), extra], axis=0).astype(BF16)
    pl.semaphore_wait(barrier, NB - 1 + NE - 1)

    def send(src, dst, ssem, rsem, db, de):
        pltpu.make_async_remote_copy(
            src_ref=src, dst_ref=dst, send_sem=ssem, recv_sem=rsem, device_id=(db, de), device_id_type=MESH
        ).start()

    def a2a_start(src, dst, ssem, rsem):
        dst[b] = src[b]

        def one(i, carry):
            to = (b + i) % NB
            send(src.at[to], dst.at[b], ssem, rsem, to, e)
            return carry

        lax.fori_loop(1, NB, one, 0)

    def a2a_wait(dst, rsem):
        wait_bytes(dst.at[pl.ds(0, NB - 1)], rsem)

    def step(i, sign):
        group = i // 8
        along = (2 * group + 1 + 3 * (group // 2)) % 4
        return ((yh + 4 + sign * along) % 4) * 8 + (b % 8 + 8 + sign * (i % 8)) % 8

    def dispatch(src, dst, ssem, rsems):
        def one(i, carry):
            to = step(i, 1)
            send(src.at[to], dst.at[i], ssem, rsems.at[i // SET], to, e)
            return carry

        lax.fori_loop(0, SET, one, 0)
        dst[SET] = src[b]
        lax.fori_loop(SET + 1, NB, one, 0)

    def dispatch_wait(dst, rsems, which):
        wait_bytes(dst.at[pl.ds(0, SET - which)], rsems.at[which])

    def packed(landed, which):
        rows = landed[pl.ds(which * SET, SET)].reshape(SET * SLOT, COLS)
        return mm(cmat[...], rows).astype(BF16)

    def to_experts(src_of, dst, ssem, rsem):
        def one(i, carry):
            to = (e + i) % NE
            send(src_of(to), dst.at[e], ssem, rsem, b, to)
            return carry

        lax.fori_loop(1, NE, one, 0)

    def to_z(src, dst, ssem, rsem):
        def one(i, carry):
            to = (z + i) % NZ
            send(src, dst.at[z], ssem, rsem, b, zdev(to))
            return carry

        lax.fori_loop(1, NZ, one, 0)

    def ring_gather(buf, ssem, rsems, first, size):
        def piece(src, half):
            return buf.at[src, pl.ds(first + half * size, size)]

        for k in range(5):
            for way, half, far in STREAMS:
                if k > far:
                    continue
                src = (z + 8 - way * k) % NZ
                if k > 0:
                    wait_bytes(piece(src, half), rsems.at[src * 2 + half])
                if k < far:
                    send(piece(src, half), piece(src, half), ssem, rsems.at[src * 2 + half], b, zdev((z + 8 + way) % NZ))
            yield k

    def ring_reduce(term, out, inn, ssem, rsems):
        for d in range(4, 0, -1):
            right = term((z + d) % NZ)
            terms = {1: right, -1: right if d == 4 else term((z + 8 - d) % NZ)}
            for starts in (True, False):
                for index, (way, half, far) in enumerate(STREAMS):
                    if d > far or starts != (d == far):
                        continue
                    value = terms[way][half * QUARTER : (half + 1) * QUARTER]
                    here = index * 5 + d
                    if d < far:
                        wait_bytes(inn.at[here], rsems.at[here])
                        value = value + inn[here].astype(F32)
                    out[here] = value.astype(BF16)
                    send(out.at[here], inn.at[here - 1], ssem, rsems.at[here - 1], b, zdev((z + 8 + way) % NZ))
            yield None
        own = term(z)
        for index in range(4):
            wait_bytes(inn.at[index * 5], rsems.at[index * 5])
        arrived = [inn[half * 5].astype(F32) + inn[(2 + half) * 5].astype(F32) for half in range(2)]
        yield own + jnp.concatenate(arrived, axis=0)

    def kv_go(block, to):
        send(kvb.at[block], kvb.at[block], kv_send.at[0], kv_recv.at[block], to, e)

    def kv_x(block):
        for dx in (1, 3, 2):
            kv_go(block, blk_of(yh, (x + dx) % 4, core))
        kv_go(block, blk_of(yh, x, 1 - core))

    for dy in (1, 3, 2):
        kv_go(b, blk_of((yh + dy) % 4, x, core))
    kv_x(b)

    for copy in locals_[4:9]:
        copy.wait()
    pi = iota((TOK, TOK), 0)
    pj = iota((TOK, TOK), 1)
    fold = jnp.where(pi == 4 * (pj & 31) + (pj >> 5), 1.0, 0.0).astype(BF16)
    row_ids = mm(ids16, jnp.where((li & 31) == ri, 1.0, 0.0).astype(BF16))
    shut = jnp.where((row16 < 3) & (row_ids != row16.astype(F32)), -1e30, 0.0)
    qp = jnp.concatenate([mm(q_in[...], fold), jnp.zeros((HD, TOK), F32), shut], axis=0).astype(BF16)
    unit = (iota((KVR, KVR), 0) == iota((KVR, KVR), 1)).astype(BF16)
    qt = mm_tn(qp, unit).astype(BF16)

    group = iota((HD, TOK), 1) >> 5
    fi = iota((HD, 4 * HD), 0)
    fj = iota((HD, 4 * HD), 1)
    gain = jnp.zeros((HD, TOK), F32)
    for i in range(4):
        column = jnp.sum(jnp.where(fj == fi + i * HD, gain_in[...], 0.0), axis=1, keepdims=True)
        gain = jnp.where(group == i, column, gain)
    gain_hi = gain_in[...].astype(BF16).astype(F32)
    gi = iota((16, 4 * HD), 0)
    gain_rows = jnp.where(gi == 0, gain_hi, jnp.where(gi == 1, gain_in[...] - gain_hi, 0.0)).astype(BF16)

    upper = (iota((TOK, TOK), 0) < iota((TOK, TOK), 1)).astype(BF16)
    ids = 2 * iota((NB, TOK), 0) + y
    hit = jnp.zeros((NB, TOK), F32)
    gate = jnp.zeros((NB, TOK), F32)
    for k in range(8):
        same = routes_in[k : k + 1, :] == ids
        hit = hit + jnp.where(same, 1.0, 0.0)
        gate = gate + jnp.where(same, gates_in[k : k + 1, :], 0.0)
    rank = mm(hit.astype(BF16), upper)
    place = jnp.where(hit > 0.0, rank, -1.0)
    slot3 = iota((NB, SLOT, TOK), 1).astype(F32)
    one_hot = jnp.where(place[:, None, :] == slot3, 1.0, 0.0)
    gated = (one_hot * gate[:, None, :]).reshape(NB * SLOT, TOK)
    dmat[...] = one_hot.reshape(NB * SLOT, TOK).astype(BF16)
    high = gated.astype(BF16)
    dg_hi[...] = high
    dg_lo[...] = (gated - high.astype(F32)).astype(BF16)
    slot_gate = jnp.sum(gated, axis=1, keepdims=True)
    locals_[9].wait()
    back = (mm(dmat[...], cot[...]) * slot_gate).astype(BF16)
    cot_out[...] = back.reshape(NB, SLOT, COLS)

    locals_[10].wait()
    gw = mm(gain_rows, mw[...])
    gw = gw[0:1, :] + gw[1:2, :]
    for c in range(NZ):
        gw_all[e, c : c + 1, :] = gw[:, c * COLS : (c + 1) * COLS]
    to_experts(lambda to: gw_all.at[e], gw_all, e_send.at[0], e_recv.at[0])

    for dy in (1, 3, 2):
        block = blk_of((yh + 4 - dy) % 4, x, core)
        wait_bytes(kvb.at[block], kv_recv.at[block])
        kv_x(block)
    dispatch(cot_out, cot_in, a2a_send.at[0], set_recv.at[0])

    ci = iota((HALF, SET * SLOT), 0)
    cj = iota((HALF, SET * SLOT), 1)
    cmat[...] = jnp.where((ci == (cj >> 4) * CAPX + (cj & 15)) & ((cj & 15) < CAPX), 1.0, 0.0).astype(BF16)

    def kv_arrive(xx, cc):
        for yy in range(4):
            block = blk_of((yh + yy) % 4, xx, cc)
            wait_bytes(kvb.at[block], kv_recv.at[block])

    def kv_pass(dx):
        def one(i, carry):
            block = blk_of((yh + 4 - i) % 4, (x + 4 - dx) % 4, core)
            wait_bytes(kvb.at[block], kv_recv.at[block])
            kv_go(block, blk_of(yh, x, 1 - core))
            return carry

        lax.fori_loop(0, 4, one, 0)

    def attend(state, xx, cc):
        top, total, acc = state
        block = jnp.concatenate([kvb[blk_of(yy, xx, cc)] for yy in range(4)], axis=1)
        s = mm(qt, block)
        new_top = jnp.maximum(top, jnp.max(s, axis=1, keepdims=True))
        shrink = jnp.exp((top - new_top) * (HD ** -0.5))
        w = jnp.exp((s - new_top) * (HD ** -0.5))
        total = total * shrink + jnp.sum(w, axis=1, keepdims=True)
        return new_top, total, acc * shrink + mm_nt(w.astype(BF16), block)

    state = (jnp.full((TOK, 1), -1e30, F32), jnp.zeros((TOK, 1), F32), jnp.zeros((TOK, KVR), F32))
    state = attend(state, x, core)
    kv_pass(1)
    kv_arrive(x, 1 - core)
    state = attend(state, x, 1 - core)
    kv_pass(3)
    state = attend(state, (x + 3) % 4, core)
    kv_pass(2)
    kv_arrive((x + 3) % 4, 1 - core)
    state = attend(state, (x + 3) % 4, 1 - core)
    state = attend(state, (x + 1) % 4, core)
    kv_arrive((x + 1) % 4, 1 - core)
    state = attend(state, (x + 1) % 4, 1 - core)
    for which in range(2):
        dispatch_wait(cot_in, set_recv.at[0], which)
        xc[z, pl.ds(which * HALF, HALF), :] = packed(cot_in, which)
    cot_ring = ring_gather(xc, ring_send.at[0], ring_recv.at[0], 0, HALF)
    next(cot_ring)
    state = attend(state, (x + 2) % 4, core)
    kv_arrive((x + 2) % 4, 1 - core)
    _, total, acc = attend(state, (x + 2) % 4, 1 - core)
    pick = (iota((HD, KVR), 1) == iota((HD, KVR), 0) + HD).astype(BF16)
    attn = mm_nt(pick, (acc / total).astype(BF16))

    def over_i(row):
        row = row + pltpu.roll(row, 32, 1)
        return row + pltpu.roll(row, 64, 1)

    local_mean = over_i(jnp.broadcast_to(jnp.sum(attn, axis=0, keepdims=True), (8, TOK)))[0:1, :] * (1.0 / (4 * HD))
    centred = attn - local_mean
    squares = over_i(jnp.broadcast_to(jnp.sum(centred * centred, axis=0, keepdims=True), (8, TOK)))
    st_all[e] = jnp.where(iota((8, TOK), 0) == 0, local_mean, squares)
    to_experts(lambda to: st_all.at[e], st_all, e_send.at[1], e_recv.at[1])
    scaled = centred * gain
    left = jnp.concatenate([jnp.where(group == i, scaled, 0.0) for i in range(4)], axis=0).astype(BF16)

    def merge_chunk(c):
        cols = pl.ds(pl.multiple_of(c * COLS, COLS), COLS)
        v = mm_tn(left, mw[:, cols])
        vp[c] = (v[0:32] + v[32:64] + v[64:96] + v[96:128]).astype(BF16)

    def merge_send(i, carry):
        c = (z + 1 + i) % NZ
        merge_chunk(c)
        send(vp.at[c], vp_all.at[e], e_send.at[2], e_recv.at[2], b, c)
        send(vp.at[c], vp_all.at[e], e_send.at[2], e_recv.at[2], b, NZ + c)
        return carry

    lax.fori_loop(0, NZ - 1, merge_send, 0)
    merge_chunk(z)
    vp_all[e] = vp[z]
    send(vp.at[z], vp_all.at[e], e_send.at[2], e_recv.at[2], b, (1 - y) * NZ + z)

    places = kvb[:, 144:160, :].astype(F32)
    places = jnp.sum(jnp.where(iota((NB, 16, TOK), 1) == 3, places, 0.0), axis=1)
    named = jnp.where(places == b.astype(F32), 1.0, 0.0)
    count = jnp.broadcast_to(jnp.sum(named, axis=1, keepdims=True), (NB, TOK))
    below = (iota((NB, NB), 1) < iota((NB, NB), 0)).astype(BF16)
    base = mm(below, count.astype(BF16))
    placed = jnp.sum(count, axis=0, keepdims=True)[:, 0:1]
    q3 = iota((NB, 8, TOK), 1).astype(F32)
    k3 = jnp.where(q3 < 4.0, q3, q3 - 4.0)
    lane3 = iota((NB, 8, TOK), 2).astype(F32)
    mine = jnp.where((lane3 == base[:, None, :] + k3) & (k3 < count[:, None, :]), 1.0, 0.0)
    ga[...] = jnp.where(q3 < 4.0, mine, 0.0).reshape(NB * 8, TOK).astype(BF16)
    gb[...] = jnp.where(q3 < 4.0, 0.0, mine).reshape(NB * 8, TOK).astype(BF16)
    to_shard = jnp.where(place_row == iota((NB, TOK), 0).astype(F32), 1.0, 0.0)
    order = mm(to_shard.astype(BF16), upper)
    order = jnp.where(to_shard > 0.0, order, -1.0)
    theirs = jnp.where(order[:, None, :] == k3, 1.0, 0.0)
    sa[...] = jnp.where(q3 < 4.0, theirs, 0.0).reshape(NB * 8, TOK).astype(BF16)
    sb[...] = jnp.where(q3 < 4.0, 0.0, theirs).reshape(NB * 8, TOK).astype(BF16)

    cv_out[...] = (mm(ga[...], cot[:, 0:TOK]) + mm(gb[...], cot[:, TOK:COLS])).reshape(NB, 8, TOK)
    a2a_start(cv_out, cv_in, row_send.at[0], row_recv.at[0])

    wait_bytes(gw_all.at[pl.ds(0, NE - 1)], e_recv.at[0])
    wait_bytes(st_all.at[pl.ds(0, NE - 1)], e_recv.at[1])
    row_stats = st_all[...]
    first = iota((NE, 8, TOK), 1) == 0
    means = jnp.sum(jnp.where(first, row_stats, 0.0), axis=1)
    mean = jnp.sum(means, axis=0, keepdims=True) * (1.0 / NE)
    spread = means - mean
    inner = jnp.sum(row_stats[:, 1:2, :], axis=0)
    variance = (inner + jnp.sum(spread * spread, axis=0, keepdims=True) * (4.0 * HD)) * (1.0 / MERGE)
    inv_std = lax.rsqrt(variance + EPS)
    normed = (attn - mean) * inv_std
    here_z = iota((NE, NZ, COLS), 1) == z
    gw_slice = jnp.sum(jnp.where(here_z, gw_all[...], 0.0), axis=1)
    shift = lax.dot_general(
        spread, gw_slice, (((0,), (0,)), ((), ())), preferred_element_type=F32, precision=lax.Precision.HIGHEST
    )[0:MR]
    inv_column = jnp.sum(jnp.where(pi == pj, inv_std, 0.0), axis=1, keepdims=True)[0:MR]
    wait_bytes(vp_all.at[pl.ds(0, NE - 1)], e_recv.at[2])
    next(cot_ring)
    vision = ((jnp.sum(vp_all[...].astype(F32), axis=0) + shift) * inv_column).astype(BF16)
    vis_all[z] = vision
    fill = jnp.zeros((TOK - MR, COLS), BF16)
    padded = jnp.concatenate([vision, fill], axis=0)
    vi_out[...] = (mm(sa[...], padded[:, 0:TOK]) + mm(sb[...], padded[:, TOK:COLS])).reshape(NB, 8, TOK)
    a2a_start(vi_out, vi_in, row_send.at[1], row_recv.at[1])
    to_z(vis_all.at[z], vis_all, z_send.at[0], z_recv.at[0])

    locals_[12].wait()
    locals_[13].wait()

    def gain_chunk(c, carry):
        cols = pl.ds(pl.multiple_of(c * COLS, COLS), COLS)
        g = ng_ref[:, cols]
        wgs[:, cols] = (wg[:, cols].astype(F32) * g).astype(BF16)
        wus[:, cols] = (wu[:, cols].astype(F32) * g).astype(BF16)
        return carry

    lax.fori_loop(0, NZ, gain_chunk, 0)
    next(cot_ring)
    a2a_wait(cv_in, row_recv.at[0])
    cv = cv_in[...].reshape(NB * 8, TOK).astype(BF16)
    cv_all[z, :, 0:TOK] = mm_tn(sa[...], cv)[0:MR].astype(BF16)
    cv_all[z, :, TOK:COLS] = mm_tn(sb[...], cv)[0:MR].astype(BF16)
    to_z(cv_all.at[z], cv_all, z_send.at[1], z_recv.at[1])

    locals_[11].wait()
    a2a_wait(vi_in, row_recv.at[1])
    arrived = vi_in[...].reshape(NB * 8, TOK).astype(BF16)
    taken = iota((TOK, TOK), 0).astype(F32) < placed
    llm_a = jnp.where(taken, mm_tn(ga[...], arrived), text[:, 0:TOK].astype(F32))
    llm_b = jnp.where(taken, mm_tn(gb[...], arrived), text[:, TOK:COLS].astype(F32))
    text[:, 0:TOK] = llm_a.astype(BF16)
    text[:, TOK:COLS] = llm_b.astype(BF16)
    h_out[...] = mm(dmat[...], text[...]).astype(BF16).reshape(NB, SLOT, COLS)
    dispatch(h_out, h_in, a2a_send.at[1], set_recv.at[1])

    for _ in cot_ring:
        pass
    locals_[14].wait()
    act_grad[...] = jnp.zeros_like(act_grad)
    gate_acc[...] = jnp.zeros_like(gate_acc)
    up_acc[...] = jnp.zeros_like(up_acc)
    ss_acc[...] = jnp.zeros_like(ss_acc)

    def act_chunk(c, carry):
        cols = pl.ds(pl.multiple_of(c * COLS, COLS), COLS)
        act_grad[...] += mm_nt(xc[c], wd[:, cols])
        return carry

    lax.fori_loop(0, NZ, act_chunk, 0)

    def project(c, which):
        cols = pl.ds(pl.multiple_of(c * COLS, COLS), COLS)
        part = pl.ds(which * HALF, HALF)
        rows = xh[c, part, :]
        gate_acc[part, :] += mm_nt(rows, wgs[:, cols])
        up_acc[part, :] += mm_nt(rows, wus[:, cols])
        wide = rows.astype(F32)
        ss_acc[part, :] += wide[:, 0:TOK] * wide[:, 0:TOK] + wide[:, TOK:COLS] * wide[:, TOK:COLS]

    h_rings = [
        ring_gather(xh, ring_send.at[1 + which], ring_recv.at[1 + which], which * HALF, QUARTER) for which in range(2)
    ]

    def h_round(k, which):
        if k == 0:
            dispatch_wait(h_in, set_recv.at[1], which)
            xh[z, pl.ds(which * HALF, HALF), :] = packed(h_in, which)
        next(h_rings[which])
        project((z + k) % NZ, which)
        if 0 < k < 4:
            project((z + 8 - k) % NZ, which)

    def hidden_units(which):
        part = pl.ds(which * HALF, HALF)
        inv = lax.rsqrt(jnp.sum(ss_acc[part, :], axis=1, keepdims=True) * (1.0 / WIDTH) + EPS)
        gate_pre = gate_acc[part, :] * inv
        up_proj = up_acc[part, :] * inv
        sig = 1.0 / (1.0 + jnp.exp(-gate_pre))
        grad = act_grad[part, :]
        hidden[0, part, :] = (grad * up_proj * sig * (1.0 + gate_pre * (1.0 - sig))).astype(BF16)
        hidden[1, part, :] = (grad * gate_pre * sig).astype(BF16)
        hidden[2, part, :] = (gate_pre * sig * up_proj).astype(BF16)

    def reducers(which):
        part = pl.ds(which * HALF, HALF)

        def grad_term(c):
            cols = pl.ds(pl.multiple_of(c * COLS, COLS), COLS)
            return mm(hidden[0, part, :], wg[:, cols]) + mm(hidden[1, part, :], wu[:, cols])

        def down_term(c):
            cols = pl.ds(pl.multiple_of(c * COLS, COLS), COLS)
            return mm(hidden[2, part, :], wd[:, cols])

        return [
            ring_reduce(term, rs_out.at[2 * which + j], rs_in.at[2 * which + j], rs_send.at[0], rs_recv.at[2 * which + j])
            for j, term in enumerate((down_term, grad_term))
        ]

    rings = [reducers(which) for which in range(2)]

    def reduce_round(which):
        for ring in rings[which]:
            next(ring)

    def give_back(which):
        for j, (out, inn) in enumerate(((dn_out, dn_in), (rg_out, rg_in))):
            rows = next(rings[which][j]).astype(BF16)
            out[pl.ds(which * SET, SET)] = mm_tn(cmat[...], rows).astype(BF16).reshape(SET, SLOT, COLS)
            if which == 1:
                inn[b] = out[SET]

            def one(i, carry):
                to = step(i, -1)
                send(out.at[i], inn.at[b], a2a_send.at[2 + j], a2a_recv.at[j], to, e)
                return carry

            lax.fori_loop(which * (SET + 1), SET + which * SET, one, 0)

    for k in range(4):
        h_round(k, 0)
        h_round(k, 1)
    h_round(4, 0)
    hidden_units(0)
    reduce_round(0)
    h_round(4, 1)
    hidden_units(1)
    reduce_round(0)
    reduce_round(1)
    reduce_round(0)
    reduce_round(1)
    reduce_round(0)
    reduce_round(1)
    give_back(0)
    reduce_round(1)
    give_back(1)

    a2a_wait(dn_in, a2a_recv.at[0])
    dn = dn_in[...].reshape(NB * SLOT, COLS)
    mine_sum = mm_tn(dg_hi[...], dn) + mm_tn(dg_lo[...], dn)
    pair_out[...] = mine_sum.astype(BF16)
    send(pair_out, pair_in, pair_send.at[0], pair_recv.at[0], b, (1 - y) * NZ + z)

    a2a_wait(rg_in, a2a_recv.at[1])
    token_grad = mm_tn(dmat[...], rg_in[...].reshape(NB * SLOT, COLS)).astype(BF16)
    hg_out[...] = (mm(ga[...], token_grad[:, 0:TOK]) + mm(gb[...], token_grad[:, TOK:COLS])).reshape(NB, 8, TOK)
    a2a_start(hg_out, hg_in, row_send.at[2], row_recv.at[2])

    wait_bytes(pair_in, pair_recv.at[0])
    layer = pair_out[...].astype(F32) + pair_in[...].astype(F32)
    llm_all[z] = (text[...].astype(F32) + layer).astype(BF16)
    llm_ring = ring_gather(llm_all, llm_send.at[0], llm_recv.at[0], 0, TOK // 2)
    next(llm_ring)
    next(llm_ring)
    next(llm_ring)
    a2a_wait(hg_in, row_recv.at[2])
    hg = hg_in[...].reshape(NB * 8, TOK).astype(BF16)
    hg_mine[:, 0:TOK] = mm_tn(sa[...], hg)[0:MR].astype(BF16)
    hg_mine[:, TOK:COLS] = mm_tn(sb[...], hg)[0:MR].astype(BF16)
    hg_all[e] = hg_mine[...]
    to_experts(lambda to: hg_mine, hg_all, e_send.at[3], e_recv.at[3])

    wait_bytes(vis_all.at[pl.ds(0, NZ - 1)], z_recv.at[0])
    wait_bytes(cv_all.at[pl.ds(0, NZ - 1)], z_recv.at[1])
    wait_bytes(hg_all.at[pl.ds(0, NE - 1)], e_recv.at[3])

    gw_sum = jnp.sum(gw_all[...], axis=0)
    ssq = jnp.zeros((MR, COLS), F32)
    cross = jnp.zeros((MR, COLS), F32)
    for c in range(NZ):
        v = vis_all[c].astype(F32)
        ghg = (hg_all[c].astype(F32) + hg_all[NZ + c].astype(F32)) * ng_ref[:, c * COLS : (c + 1) * COLS]
        ssq = ssq + v * v
        cross = cross + ghg * v
    r = lax.rsqrt(jnp.sum(ssq, axis=1, keepdims=True) * (1.0 / WIDTH) + EPS)
    pull = jnp.sum(cross, axis=1, keepdims=True) * (1.0 / WIDTH) * r * r * r
    dot_g = jnp.zeros((MR, COLS), F32)
    dot_v = jnp.zeros((MR, COLS), F32)
    back_scaled = jnp.zeros((4 * HD, TOK), F32)
    for c in range(NZ):
        v = vis_all[c].astype(F32)
        ghg = (hg_all[c].astype(F32) + hg_all[NZ + c].astype(F32)) * ng_ref[:, c * COLS : (c + 1) * COLS]
        vg = (cv_all[c].astype(F32) + (r * ghg - v * pull)).astype(BF16)
        wide = vg.astype(F32)
        dot_g = dot_g + wide * gw_sum[c : c + 1, :]
        dot_v = dot_v + wide * v
        four = jnp.concatenate([vg, vg, vg, vg], axis=0)
        back_scaled = back_scaled + mm_nt(mw[:, c * COLS : (c + 1) * COLS], four)
    next(llm_ring)

    def to_lanes(columns):
        column = jnp.sum(columns, axis=1, keepdims=True)
        column = jnp.concatenate([column, column, column, column], axis=0)
        eye = iota((TOK, TOK), 0) == iota((TOK, TOK), 1)
        return jnp.sum(jnp.where(eye, column, 0.0), axis=0, keepdims=True)

    grad_mean = to_lanes(dot_g) * (1.0 / MERGE)
    cross_mean = to_lanes(dot_v) * (1.0 / MERGE)
    scaled_grad = jnp.zeros((HD, TOK), F32)
    for i in range(4):
        scaled_grad = jnp.where(group == i, back_scaled[i * HD : (i + 1) * HD, :], scaled_grad)
    merged_grad = inv_std * (scaled_grad * gain - grad_mean - normed * cross_mean)
    unfold = jnp.where(pj == 4 * (pi & 31) + (pi >> 5), 1.0, 0.0).astype(BF16)
    part1 = merged_grad.astype(BF16)
    rest = merged_grad - part1.astype(F32)
    part2 = rest.astype(BF16)
    part3 = (rest - part2.astype(F32)).astype(BF16)
    ag_ref[...] = mm(part1, unfold) + mm(part2, unfold) + mm(part3, unfold)
    for _ in llm_ring:
        pass
    for c in range(NZ):
        llm_ref[:, c * COLS : (c + 1) * COLS] = llm_all[c]

    wait_bytes(kvb.at[pl.ds(0, NB - 1)], kv_send.at[0])
    for index, buf in enumerate((cot_out, h_out, dn_out, rg_out)):
        wait_bytes(buf.at[pl.ds(0, NB - 1)], a2a_send.at[index])
    for index, buf in enumerate((cv_out, vi_out, hg_out)):
        wait_bytes(buf.at[pl.ds(0, NB - 1)], row_send.at[index])
    for index, buf in enumerate((gw_all, st_all, vp_all, hg_all)):
        wait_bytes(buf.at[pl.ds(0, NE - 1)], e_send.at[index])
    for index, buf in enumerate((vis_all, cv_all)):
        wait_bytes(buf.at[pl.ds(0, NZ - 1)], z_send.at[index])
    wait_bytes(xc.at[pl.ds(0, NZ - 1)], ring_send.at[0])
    for index in range(2):
        wait_bytes(xh.at[pl.ds(0, NZ - 1), pl.ds(0, HALF)], ring_send.at[1 + index])
    wait_bytes(rs_out.at[:, pl.ds(0, 14)], rs_send.at[0])
    wait_bytes(pair_out, pair_send.at[0])
    wait_bytes(llm_all.at[pl.ds(0, NZ - 1)], llm_send.at[0])


def scratch_shapes():
    V = pltpu.VMEM
    D = pltpu.SemaphoreType.DMA
    routed = [V((NB, SLOT, COLS), BF16)] * 8
    rows = [V((NB, 8, TOK), F32)] * 6
    return (
        [V((HD, TOK), BF16)] * 3
        + [V((1, MR), jnp.int32), V((1, MR), jnp.int32), V((1, 4 * HD), F32), V((1, WIDTH), F32)]
        + [V((8, TOK), jnp.int32), V((8, TOK), F32)]
        + [V((4 * HD, WIDTH), BF16), V((TOK, COLS), BF16), V((TOK, COLS), BF16)]
        + [V((FG, WIDTH), BF16)] * 5
        + [D((15,))]
        + [V((NB, KVR, TOK), BF16), D((1,)), D((NB,))]
        + [V((NB * SLOT, TOK), BF16)] * 3
        + [V((HALF, SET * SLOT), BF16)]
        + [V((NB * 8, TOK), BF16)] * 4
        + routed + [D((4,)), D((2,)), D((2, 2))]
        + rows + [D((3,)), D((3,))]
        + [V((NE, NZ, COLS), F32), V((NE, 8, TOK), F32), V((NZ, MR, COLS), BF16), V((NE, MR, COLS), BF16)]
        + [V((NE, MR, COLS), BF16), V((MR, COLS), BF16), D((4,)), D((4,))]
        + [V((NZ, MR, COLS), BF16)] * 2 + [D((2,)), D((2,))]
        + [V((NZ, ROWS, COLS), BF16)] * 2 + [D((3,)), D((3, 16))]
        + [V((ROWS, FG), F32), V((ROWS, FG), F32), V((ROWS, TOK), F32), V((ROWS, FG), F32), V((3, ROWS, FG), BF16)]
        + [V((4, 20, QUARTER, COLS), BF16)] * 2 + [D((1,)), D((4, 20))]
        + [V((TOK, COLS), BF16)] * 2 + [D((1,)), D((1,))]
        + [V((NZ, TOK, COLS), BF16), D((1,)), D((1, 16))]
    )


def body(
    queries, keys, values, image_ids, placement, merge_gain, merge_weight, text, norm_gain,
    w_gate, w_up, w_down, routes, route_gates, cotangent,
):
    vm = pl.BlockSpec(memory_space=pltpu.VMEM)
    anywhere = pl.BlockSpec(memory_space=pl.ANY)
    llm_out, attn_grad = pl.pallas_call(
        kernel,
        out_shape=(
            jax.ShapeDtypeStruct((TOK, WIDTH), BF16),
            jax.ShapeDtypeStruct((HD, TOK), F32),
        ),
        in_specs=[anywhere] * 15,
        out_specs=(vm, vm),
        scratch_shapes=scratch_shapes(),
        compiler_params=pltpu.CompilerParams(
            collective_id=0, has_side_effects=True, vmem_limit_bytes=VMEM_BYTES
        ),
    )(
        queries, keys, values, image_ids[None, :], placement.T, merge_gain, merge_weight, text, norm_gain[None, :],
        w_gate, w_up, w_down, routes.T, route_gates.T, cotangent,
    )
    return llm_out, attn_grad[None]


def solution(mesh):
    return jax.shard_map(
        body,
        mesh=mesh,
        in_specs=(
            P("expert", None, "blk"),
            P("expert", None, "blk"),
            P("expert", None, "blk"),
            P("blk"),
            P("blk", None),
            P("expert", None),
            P("expert", None, None),
            P("blk", None),
            P(),
            P("blk", "expert", None),
            P("blk", "expert", None),
            P("blk", "expert", None),
            P("blk", None),
            P("blk", None),
            P("blk", None),
        ),
        out_specs=(P("blk", None), P("expert", None, "blk")),
        check_vma=False,
    )
```

time: 183 us -> 147 us (0.80)
  the two profiles are of different devices: /device:TPU:8 before, /device:TPU:48 now
where the time goes in v2:
time: 147 us
  Pallas kernels  143 us (97%)
  local copies, waits for them, and re-layouts  3.27 us (2%)
    pallas_call x1, Pallas kernels, body(): pl.pallas_call(kernel, out_shape=(jax.ShapeDtypeStruct((TOK, WIDTH), BF16...  143 us
    unnamed x2, local copies, waits for them, and re-layouts  3.27 us

profile of v2, /device:TPU:48, one launch (start us, length us, event | category | flops | bytes accessed | tf_op | source)
XLA Modules:
  0.0 147.2 jit_solution(1415976671739436598)
XLA Ops:
  0.6 143.3 %shard_map.158 = (bf16[128,2048]{1,0:T(8,128)(2,1)}, f32[72,128]{1,0:T(8,128)}) custom-call(bf16[1,72,128]{2,1,0:T(8,128)(2,1)} %q_hbm.1, bf16[1,72,128]{2,1,0:T(8,128)(2,1)} %k_hbm.1, bf16[1,72,128]{2,1,0:T(8,128)(2,1)} %v_hbm.1, s32[1,32]{1,0:T(1,128)} %bitcast.10, s32[1,32]{1,0:T(1,128)} %bitcast.11, f32[1,288]{1,0:T(1,128)} %gain_hbm.1, ...), custom_call_target="tpu_custom_call" | custom-call | tf_op jit(solution)/shard_map/pallas_call | solution.py:676
  143.9 1.9 %copy.19 = bf16[128,2048]{1,0:T(8,128)(2,1)} copy(bf16[128,2048]{1,0:T(8,128)(2,1)} %get-tuple-element.8) | data formatting | bytes 1048576
  145.8 1.4 copy.20

commit v3 on v2

--- a/solution.py
+++ b/solution.py
@@ -139,20 +139,23 @@
     def a2a_wait(dst, rsem):
         wait_bytes(dst.at[pl.ds(0, NB - 1)], rsem)
 
-    def step(i, sign):
-        group = i // 8
-        along = (2 * group + 1 + 3 * (group // 2)) % 4
-        return ((yh + 4 + sign * along) % 4) * 8 + (b % 8 + 8 + sign * (i % 8)) % 8
+    within = lax.rem(b, 8)
+
+    def steps(which, sign, go):
+        for group in (0, 1):
+            along = ((1, 3), (0, 2))[which][group]
+            base = lax.rem(yh + 4 + sign * along, 4) * 8
+
+            def one(j, carry):
+                go(which * SET + group * 8 + j, base + lax.rem(within + 8 + sign * j, 8))
+                return carry
+
+            lax.fori_loop(0 if along > 0 else 1, 8, one, 0)
 
     def dispatch(src, dst, ssem, rsems):
-        def one(i, carry):
-            to = step(i, 1)
-            send(src.at[to], dst.at[i], ssem, rsems.at[i // SET], to, e)
-            return carry
-
-        lax.fori_loop(0, SET, one, 0)
+        for which in (0, 1):
+            steps(which, 1, lambda i, to: send(src.at[to], dst.at[i], ssem, rsems.at[which], to, e))
         dst[SET] = src[b]
-        lax.fori_loop(SET + 1, NB, one, 0)
 
     def dispatch_wait(dst, rsems, which):
         wait_bytes(dst.at[pl.ds(0, SET - which)], rsems.at[which])
@@ -269,6 +272,7 @@
     locals_[9].wait()
     back = (mm(dmat[...], cot[...]) * slot_gate).astype(BF16)
     cot_out[...] = back.reshape(NB, SLOT, COLS)
+    dispatch(cot_out, cot_in, a2a_send.at[0], set_recv.at[0])
 
     locals_[10].wait()
     gw = mm(gain_rows, mw[...])
@@ -281,7 +285,6 @@
         block = blk_of((yh + 4 - dy) % 4, x, core)
         wait_bytes(kvb.at[block], kv_recv.at[block])
         kv_x(block)
-    dispatch(cot_out, cot_in, a2a_send.at[0], set_recv.at[0])
 
     ci = iota((HALF, SET * SLOT), 0)
     cj = iota((HALF, SET * SLOT), 1)
@@ -319,16 +322,16 @@
     kv_pass(3)
     state = attend(state, (x + 3) % 4, core)
     kv_pass(2)
+    for which in range(2):
+        dispatch_wait(cot_in, set_recv.at[0], which)
+        xc[z, pl.ds(which * HALF, HALF), :] = packed(cot_in, which)
+    cot_ring = ring_gather(xc, ring_send.at[0], ring_recv.at[0], 0, HALF)
+    next(cot_ring)
     kv_arrive((x + 3) % 4, 1 - core)
     state = attend(state, (x + 3) % 4, 1 - core)
     state = attend(state, (x + 1) % 4, core)
     kv_arrive((x + 1) % 4, 1 - core)
     state = attend(state, (x + 1) % 4, 1 - core)
-    for which in range(2):
-        dispatch_wait(cot_in, set_recv.at[0], which)
-        xc[z, pl.ds(which * HALF, HALF), :] = packed(cot_in, which)
-    cot_ring = ring_gather(xc, ring_send.at[0], ring_recv.at[0], 0, HALF)
-    next(cot_ring)
     state = attend(state, (x + 2) % 4, core)
     kv_arrive((x + 2) % 4, 1 - core)
     _, total, acc = attend(state, (x + 2) % 4, 1 - core)
@@ -347,22 +350,33 @@
     scaled = centred * gain
     left = jnp.concatenate([jnp.where(group == i, scaled, 0.0) for i in range(4)], axis=0).astype(BF16)
 
-    def merge_chunk(c):
-        cols = pl.ds(pl.multiple_of(c * COLS, COLS), COLS)
-        v = mm_tn(left, mw[:, cols])
-        vp[c] = (v[0:32] + v[32:64] + v[64:96] + v[96:128]).astype(BF16)
-
-    def merge_send(i, carry):
-        c = (z + 1 + i) % NZ
-        merge_chunk(c)
-        send(vp.at[c], vp_all.at[e], e_send.at[2], e_recv.at[2], b, c)
-        send(vp.at[c], vp_all.at[e], e_send.at[2], e_recv.at[2], b, NZ + c)
+    unit128 = (pi == pj).astype(BF16)
+    left = mm_nt(unit128, left).astype(BF16)
+
+    def merge_pair(j):
+        cols = pl.ds(pl.multiple_of(j * (2 * COLS), 2 * COLS), 2 * COLS)
+        v = mm(left, mw[:, cols])
+        v = (v[0:32] + v[32:64] + v[64:96] + v[96:128]).astype(BF16)
+        vp[2 * j] = v[:, 0:COLS]
+        vp[2 * j + 1] = v[:, COLS : 2 * COLS]
+
+    def merge_send(c, member):
+        send(vp.at[c], vp_all.at[e], e_send.at[2], e_recv.at[2], b, member * NZ + c)
+
+    def merge_others(i, carry):
+        j = (z // 2 + 1 + i) % 4
+        merge_pair(j)
+        for c in (2 * j, 2 * j + 1):
+            merge_send(c, 0)
+            merge_send(c, 1)
         return carry
 
-    lax.fori_loop(0, NZ - 1, merge_send, 0)
-    merge_chunk(z)
+    lax.fori_loop(0, 3, merge_others, 0)
+    merge_pair(z // 2)
+    merge_send(z + 1 - 2 * (z % 2), 0)
+    merge_send(z + 1 - 2 * (z % 2), 1)
+    merge_send(z, 1 - y)
     vp_all[e] = vp[z]
-    send(vp.at[z], vp_all.at[e], e_send.at[2], e_recv.at[2], b, (1 - y) * NZ + z)
 
     places = kvb[:, 144:160, :].astype(F32)
     places = jnp.sum(jnp.where(iota((NB, 16, TOK), 1) == 3, places, 0.0), axis=1)
@@ -456,8 +470,6 @@
         act_grad[...] += mm_nt(xc[c], wd[:, cols])
         return carry
 
-    lax.fori_loop(0, NZ, act_chunk, 0)
-
     def project(c, which):
         cols = pl.ds(pl.multiple_of(c * COLS, COLS), COLS)
         part = pl.ds(which * HALF, HALF)
@@ -504,7 +516,7 @@
 
         return [
             ring_reduce(term, rs_out.at[2 * which + j], rs_in.at[2 * which + j], rs_send.at[0], rs_recv.at[2 * which + j])
-            for j, term in enumerate((down_term, grad_term))
+            for j, term in enumerate((grad_term, down_term))
         ]
 
     rings = [reducers(which) for which in range(2)]
@@ -514,20 +526,17 @@
             next(ring)
 
     def give_back(which):
-        for j, (out, inn) in enumerate(((dn_out, dn_in), (rg_out, rg_in))):
+        for j, (out, inn) in enumerate(((rg_out, rg_in), (dn_out, dn_in))):
             rows = next(rings[which][j]).astype(BF16)
             out[pl.ds(which * SET, SET)] = mm_tn(cmat[...], rows).astype(BF16).reshape(SET, SLOT, COLS)
             if which == 1:
                 inn[b] = out[SET]
-
-            def one(i, carry):
-                to = step(i, -1)
-                send(out.at[i], inn.at[b], a2a_send.at[2 + j], a2a_recv.at[j], to, e)
-                return carry
-
-            lax.fori_loop(which * (SET + 1), SET + which * SET, one, 0)
-
-    for k in range(4):
+            steps(which, -1, lambda i, to: send(out.at[i], inn.at[b], a2a_send.at[2 + j], a2a_recv.at[j], to, e))
+
+    h_round(0, 0)
+    h_round(0, 1)
+    lax.fori_loop(0, NZ, act_chunk, 0)
+    for k in range(1, 4):
         h_round(k, 0)
         h_round(k, 1)
     h_round(4, 0)
@@ -535,40 +544,56 @@
     reduce_round(0)
     h_round(4, 1)
     hidden_units(1)
-    reduce_round(0)
-    reduce_round(1)
-    reduce_round(0)
-    reduce_round(1)
-    reduce_round(0)
-    reduce_round(1)
+    for which in (0, 1, 0, 1, 0, 1):
+        reduce_round(which)
     give_back(0)
     reduce_round(1)
     give_back(1)
 
-    a2a_wait(dn_in, a2a_recv.at[0])
+    a2a_wait(rg_in, a2a_recv.at[0])
+    token_grad = mm_tn(dmat[...], rg_in[...].reshape(NB * SLOT, COLS)).astype(BF16)
+    hg_out[...] = (mm(ga[...], token_grad[:, 0:TOK]) + mm(gb[...], token_grad[:, TOK:COLS])).reshape(NB, 8, TOK)
+    a2a_start(hg_out, hg_in, row_send.at[2], row_recv.at[2])
+
+    a2a_wait(dn_in, a2a_recv.at[1])
     dn = dn_in[...].reshape(NB * SLOT, COLS)
     mine_sum = mm_tn(dg_hi[...], dn) + mm_tn(dg_lo[...], dn)
     pair_out[...] = mine_sum.astype(BF16)
-    send(pair_out, pair_in, pair_send.at[0], pair_recv.at[0], b, (1 - y) * NZ + z)
-
-    a2a_wait(rg_in, a2a_recv.at[1])
-    token_grad = mm_tn(dmat[...], rg_in[...].reshape(NB * SLOT, COLS)).astype(BF16)
-    hg_out[...] = (mm(ga[...], token_grad[:, 0:TOK]) + mm(gb[...], token_grad[:, TOK:COLS])).reshape(NB, 8, TOK)
-    a2a_start(hg_out, hg_in, row_send.at[2], row_recv.at[2])
+    own_half = pl.ds(pl.multiple_of(y * (TOK // 2), TOK // 2), TOK // 2)
+    other_half = pl.ds(pl.multiple_of((1 - y) * (TOK // 2), TOK // 2), TOK // 2)
+    other = (1 - y) * NZ + z
+    send(pair_out.at[other_half], pair_in, pair_send.at[0], pair_recv.at[0], b, other)
+
+    def llm_cross(src):
+        send(llm_all.at[src, own_half], llm_all.at[src, own_half], llm_send.at[1], llm_recv.at[1, src], b, other)
 
     wait_bytes(pair_in, pair_recv.at[0])
-    layer = pair_out[...].astype(F32) + pair_in[...].astype(F32)
-    llm_all[z] = (text[...].astype(F32) + layer).astype(BF16)
-    llm_ring = ring_gather(llm_all, llm_send.at[0], llm_recv.at[0], 0, TOK // 2)
-    next(llm_ring)
-    next(llm_ring)
-    next(llm_ring)
+    layer = pair_out[own_half, :].astype(F32) + pair_in[...].astype(F32)
+    llm_all[z, own_half, :] = (text[own_half, :].astype(F32) + layer).astype(BF16)
+    def llm_along(src, to):
+        part = llm_all.at[src, own_half]
+        send(part, part, llm_send.at[0], llm_recv.at[0, src], b, zdev(lax.rem(z + to, NZ)))
+
+    def llm_arrive(distance):
+        src = lax.rem(z + distance, NZ)
+        wait_bytes(llm_all.at[src, own_half], llm_recv.at[0, src])
+        return src
+
+    for to in (2, 6, 1, 7):
+        llm_along(z, to)
+    llm_cross(z)
     a2a_wait(hg_in, row_recv.at[2])
     hg = hg_in[...].reshape(NB * 8, TOK).astype(BF16)
     hg_mine[:, 0:TOK] = mm_tn(sa[...], hg)[0:MR].astype(BF16)
     hg_mine[:, TOK:COLS] = mm_tn(sb[...], hg)[0:MR].astype(BF16)
     hg_all[e] = hg_mine[...]
     to_experts(lambda to: hg_mine, hg_all, e_send.at[3], e_recv.at[3])
+
+    for distance, onward in ((6, (1, 2)), (2, (7,)), (7, ()), (1, ()), (5, ()), (3, ()), (4, ())):
+        src = llm_arrive(distance)
+        for to in onward:
+            llm_along(src, to)
+        llm_cross(src)
 
     wait_bytes(vis_all.at[pl.ds(0, NZ - 1)], z_recv.at[0])
     wait_bytes(cv_all.at[pl.ds(0, NZ - 1)], z_recv.at[1])
@@ -596,7 +621,6 @@
         dot_v = dot_v + wide * v
         four = jnp.concatenate([vg, vg, vg, vg], axis=0)
         back_scaled = back_scaled + mm_nt(mw[:, c * COLS : (c + 1) * COLS], four)
-    next(llm_ring)
 
     def to_lanes(columns):
         column = jnp.sum(columns, axis=1, keepdims=True)
@@ -616,13 +640,13 @@
     part2 = rest.astype(BF16)
     part3 = (rest - part2.astype(F32)).astype(BF16)
     ag_ref[...] = mm(part1, unfold) + mm(part2, unfold) + mm(part3, unfold)
-    for _ in llm_ring:
-        pass
+    for src in range(NZ):
+        wait_bytes(llm_all.at[src, other_half], llm_recv.at[1, src])
     for c in range(NZ):
         llm_ref[:, c * COLS : (c + 1) * COLS] = llm_all[c]
 
     wait_bytes(kvb.at[pl.ds(0, NB - 1)], kv_send.at[0])
-    for index, buf in enumerate((cot_out, h_out, dn_out, rg_out)):
+    for index, buf in enumerate((cot_out, h_out, rg_out, dn_out)):
         wait_bytes(buf.at[pl.ds(0, NB - 1)], a2a_send.at[index])
     for index, buf in enumerate((cv_out, vi_out, hg_out)):
         wait_bytes(buf.at[pl.ds(0, NB - 1)], row_send.at[index])
@@ -634,8 +658,9 @@
     for index in range(2):
         wait_bytes(xh.at[pl.ds(0, NZ - 1), pl.ds(0, HALF)], ring_send.at[1 + index])
     wait_bytes(rs_out.at[:, pl.ds(0, 14)], rs_send.at[0])
-    wait_bytes(pair_out, pair_send.at[0])
-    wait_bytes(llm_all.at[pl.ds(0, NZ - 1)], llm_send.at[0])
+    wait_bytes(pair_in, pair_send.at[0])
+    wait_bytes(llm_all.at[pl.ds(0, NZ - 1), own_half], llm_send.at[0])
+    wait_bytes(llm_all.at[:, own_half], llm_send.at[1])
 
 
 def scratch_shapes():
@@ -662,8 +687,8 @@
         + [V((NZ, ROWS, COLS), BF16)] * 2 + [D((3,)), D((3, 16))]
         + [V((ROWS, FG), F32), V((ROWS, FG), F32), V((ROWS, TOK), F32), V((ROWS, FG), F32), V((3, ROWS, FG), BF16)]
         + [V((4, 20, QUARTER, COLS), BF16)] * 2 + [D((1,)), D((4, 20))]
-        + [V((TOK, COLS), BF16)] * 2 + [D((1,)), D((1,))]
-        + [V((NZ, TOK, COLS), BF16), D((1,)), D((1, 16))]
+        + [V((TOK, COLS), BF16), V((TOK // 2, COLS), BF16), D((1,)), D((1,))]
+        + [V((NZ, TOK, COLS), BF16), D((2,)), D((2, NZ))]
     )
 
 

time: 147 us -> 139 us (0.946)
  the two profiles are of different devices: /device:TPU:48 before, /device:TPU:1 now
where the time goes in v3:
time: 139 us
  Pallas kernels  135 us (97%)
  local copies, waits for them, and re-layouts  3.27 us (2%)
    pallas_call x1, Pallas kernels, body(): pl.pallas_call(kernel, out_shape=(jax.ShapeDtypeStruct((TOK, WIDTH), BF16...  135 us
    unnamed x2, local copies, waits for them, and re-layouts  3.27 us

profile of v3, /device:TPU:1, one launch (start us, length us, event | category | flops | bytes accessed | tf_op | source)
XLA Modules:
  0.0 138.8 jit_solution(8096222460694471995)
XLA Ops:
  0.6 134.9 %shard_map.158 = (bf16[128,2048]{1,0:T(8,128)(2,1)}, f32[72,128]{1,0:T(8,128)}) custom-call(bf16[1,72,128]{2,1,0:T(8,128)(2,1)} %q_hbm.1, bf16[1,72,128]{2,1,0:T(8,128)(2,1)} %k_hbm.1, bf16[1,72,128]{2,1,0:T(8,128)(2,1)} %v_hbm.1, s32[1,32]{1,0:T(1,128)} %bitcast.10, s32[1,32]{1,0:T(1,128)} %bitcast.11, f32[1,288]{1,0:T(1,128)} %gain_hbm.1, ...), custom_call_target="tpu_custom_call" | custom-call | tf_op jit(solution)/shard_map/pallas_call | solution.py:701
  135.5 1.9 %copy.19 = bf16[128,2048]{1,0:T(8,128)(2,1)} copy(bf16[128,2048]{1,0:T(8,128)(2,1)} %get-tuple-element.8) | data formatting | bytes 1048576
  137.4 1.4 copy.20

commit v4 on v3

--- a/solution.py
+++ b/solution.py
@@ -58,9 +58,10 @@
     mw, text, cot, wg, wu, wd, wgs, wus, local_sem,
     kvb, kv_send, kv_recv,
     dmat, dg_hi, dg_lo, cmat, ga, gb, sa, sb,
-    cot_out, cot_in, h_out, h_in, rg_out, rg_in, dn_out, dn_in, a2a_send, a2a_recv, set_recv,
-    cv_out, cv_in, vi_out, vi_in, hg_out, hg_in, row_send, row_recv,
-    gw_all, st_all, vp, vp_all, hg_all, hg_mine, e_send, e_recv,
+    cot_out, cot_in, h_out, h_in, dn_out, dn_in, a2a_send, a2a_recv, set_recv,
+    by_row, core_out, core_in, x_out, x_in, y_out, y_in, sum_send, core_recv, x_recv, y_recv,
+    cv_out, cv_in, row_send, row_recv, vblk, vi_send, vi_recv, vt, pick_rows, info_out, info_in, info_send, place_all, place_recv,
+    gw_all, st_all, vp, vp_all, hg_all, hg_mine, hg_other, e_send, e_recv,
     vis_all, cv_all, z_send, z_recv,
     xc, xh, ring_send, ring_recv,
     gate_acc, up_acc, ss_acc, act_grad, hidden,
@@ -117,7 +118,7 @@
     place_row = mm(place16, jnp.where(li == ri, 1.0, 0.0).astype(BF16))[0:1, :]
     place_row = jnp.where(iota((1, TOK), 1) < MR, place_row, -1.0)
     extra = jnp.where(row16 < 3, jnp.where(patch_ids == row16.astype(F32), 1.0, 0.0), 0.0)
-    extra = jnp.where(row16 == 3, place_row, extra)
+    place_all[b] = place_row.astype(jnp.int32)
     kvb[b] = jnp.concatenate([k_in[...].astype(F32), v_in[...].astype(F32), extra], axis=0).astype(BF16)
     pl.semaphore_wait(barrier, NB - 1 + NE - 1)
 
@@ -161,8 +162,8 @@
         wait_bytes(dst.at[pl.ds(0, SET - which)], rsems.at[which])
 
     def packed(landed, which):
-        rows = landed[pl.ds(which * SET, SET)].reshape(SET * SLOT, COLS)
-        return mm(cmat[...], rows).astype(BF16)
+        rows = landed[pl.ds(which * SET, SET)].reshape(SET * SLOT, landed.shape[2])
+        return mm(cmat[...], rows)
 
     def to_experts(src_of, dst, ssem, rsem):
         def one(i, carry):
@@ -220,14 +221,41 @@
     def kv_go(block, to):
         send(kvb.at[block], kvb.at[block], kv_send.at[0], kv_recv.at[block], to, e)
 
-    def kv_x(block):
+    def vi_go(block, to):
+        send(vblk.at[block], vblk.at[block], vi_send.at[0], vi_recv.at[block], to, e)
+
+    def along_x(go, block):
         for dx in (1, 3, 2):
-            kv_go(block, blk_of(yh, (x + dx) % 4, core))
-        kv_go(block, blk_of(yh, x, 1 - core))
-
-    for dy in (1, 3, 2):
-        kv_go(b, blk_of((yh + dy) % 4, x, core))
-    kv_x(b)
+            go(block, blk_of(yh, (x + dx) % 4, core))
+        go(block, blk_of(yh, x, 1 - core))
+
+    def along_y(go):
+        for dy in (1, 3, 2):
+            go(b, blk_of((yh + dy) % 4, x, core))
+        along_x(go, b)
+
+    def onward_x(go, buf, rsems):
+        for dy in (1, 3, 2):
+            block = blk_of((yh + 4 - dy) % 4, x, core)
+            wait_bytes(buf.at[block], rsems.at[block])
+            along_x(go, block)
+
+    def onward_core(go, buf, rsems, dx):
+        def one(i, carry):
+            block = blk_of((yh + 4 - i) % 4, (x + 4 - dx) % 4, core)
+            wait_bytes(buf.at[block], rsems.at[block])
+            go(block, blk_of(yh, x, 1 - core))
+            return carry
+
+        lax.fori_loop(0, 4, one, 0)
+
+    along_y(kv_go)
+
+    def tell_place(i, carry):
+        send(place_all.at[b], place_all.at[b], info_send.at[1], place_recv.at[0], lax.rem(b + i, NB), e)
+        return carry
+
+    lax.fori_loop(1, NB, tell_place, 0)
 
     for copy in locals_[4:9]:
         copy.wait()
@@ -281,105 +309,10 @@
         gw_all[e, c : c + 1, :] = gw[:, c * COLS : (c + 1) * COLS]
     to_experts(lambda to: gw_all.at[e], gw_all, e_send.at[0], e_recv.at[0])
 
-    for dy in (1, 3, 2):
-        block = blk_of((yh + 4 - dy) % 4, x, core)
-        wait_bytes(kvb.at[block], kv_recv.at[block])
-        kv_x(block)
-
-    ci = iota((HALF, SET * SLOT), 0)
-    cj = iota((HALF, SET * SLOT), 1)
-    cmat[...] = jnp.where((ci == (cj >> 4) * CAPX + (cj & 15)) & ((cj & 15) < CAPX), 1.0, 0.0).astype(BF16)
-
-    def kv_arrive(xx, cc):
-        for yy in range(4):
-            block = blk_of((yh + yy) % 4, xx, cc)
-            wait_bytes(kvb.at[block], kv_recv.at[block])
-
-    def kv_pass(dx):
-        def one(i, carry):
-            block = blk_of((yh + 4 - i) % 4, (x + 4 - dx) % 4, core)
-            wait_bytes(kvb.at[block], kv_recv.at[block])
-            kv_go(block, blk_of(yh, x, 1 - core))
-            return carry
-
-        lax.fori_loop(0, 4, one, 0)
-
-    def attend(state, xx, cc):
-        top, total, acc = state
-        block = jnp.concatenate([kvb[blk_of(yy, xx, cc)] for yy in range(4)], axis=1)
-        s = mm(qt, block)
-        new_top = jnp.maximum(top, jnp.max(s, axis=1, keepdims=True))
-        shrink = jnp.exp((top - new_top) * (HD ** -0.5))
-        w = jnp.exp((s - new_top) * (HD ** -0.5))
-        total = total * shrink + jnp.sum(w, axis=1, keepdims=True)
-        return new_top, total, acc * shrink + mm_nt(w.astype(BF16), block)
-
-    state = (jnp.full((TOK, 1), -1e30, F32), jnp.zeros((TOK, 1), F32), jnp.zeros((TOK, KVR), F32))
-    state = attend(state, x, core)
-    kv_pass(1)
-    kv_arrive(x, 1 - core)
-    state = attend(state, x, 1 - core)
-    kv_pass(3)
-    state = attend(state, (x + 3) % 4, core)
-    kv_pass(2)
-    for which in range(2):
-        dispatch_wait(cot_in, set_recv.at[0], which)
-        xc[z, pl.ds(which * HALF, HALF), :] = packed(cot_in, which)
-    cot_ring = ring_gather(xc, ring_send.at[0], ring_recv.at[0], 0, HALF)
-    next(cot_ring)
-    kv_arrive((x + 3) % 4, 1 - core)
-    state = attend(state, (x + 3) % 4, 1 - core)
-    state = attend(state, (x + 1) % 4, core)
-    kv_arrive((x + 1) % 4, 1 - core)
-    state = attend(state, (x + 1) % 4, 1 - core)
-    state = attend(state, (x + 2) % 4, core)
-    kv_arrive((x + 2) % 4, 1 - core)
-    _, total, acc = attend(state, (x + 2) % 4, 1 - core)
-    pick = (iota((HD, KVR), 1) == iota((HD, KVR), 0) + HD).astype(BF16)
-    attn = mm_nt(pick, (acc / total).astype(BF16))
-
-    def over_i(row):
-        row = row + pltpu.roll(row, 32, 1)
-        return row + pltpu.roll(row, 64, 1)
-
-    local_mean = over_i(jnp.broadcast_to(jnp.sum(attn, axis=0, keepdims=True), (8, TOK)))[0:1, :] * (1.0 / (4 * HD))
-    centred = attn - local_mean
-    squares = over_i(jnp.broadcast_to(jnp.sum(centred * centred, axis=0, keepdims=True), (8, TOK)))
-    st_all[e] = jnp.where(iota((8, TOK), 0) == 0, local_mean, squares)
-    to_experts(lambda to: st_all.at[e], st_all, e_send.at[1], e_recv.at[1])
-    scaled = centred * gain
-    left = jnp.concatenate([jnp.where(group == i, scaled, 0.0) for i in range(4)], axis=0).astype(BF16)
-
-    unit128 = (pi == pj).astype(BF16)
-    left = mm_nt(unit128, left).astype(BF16)
-
-    def merge_pair(j):
-        cols = pl.ds(pl.multiple_of(j * (2 * COLS), 2 * COLS), 2 * COLS)
-        v = mm(left, mw[:, cols])
-        v = (v[0:32] + v[32:64] + v[64:96] + v[96:128]).astype(BF16)
-        vp[2 * j] = v[:, 0:COLS]
-        vp[2 * j + 1] = v[:, COLS : 2 * COLS]
-
-    def merge_send(c, member):
-        send(vp.at[c], vp_all.at[e], e_send.at[2], e_recv.at[2], b, member * NZ + c)
-
-    def merge_others(i, carry):
-        j = (z // 2 + 1 + i) % 4
-        merge_pair(j)
-        for c in (2 * j, 2 * j + 1):
-            merge_send(c, 0)
-            merge_send(c, 1)
-        return carry
-
-    lax.fori_loop(0, 3, merge_others, 0)
-    merge_pair(z // 2)
-    merge_send(z + 1 - 2 * (z % 2), 0)
-    merge_send(z + 1 - 2 * (z % 2), 1)
-    merge_send(z, 1 - y)
-    vp_all[e] = vp[z]
-
-    places = kvb[:, 144:160, :].astype(F32)
-    places = jnp.sum(jnp.where(iota((NB, 16, TOK), 1) == 3, places, 0.0), axis=1)
+    onward_x(kv_go, kvb, kv_recv)
+
+    wait_bytes(place_all.at[pl.ds(0, NB - 1)], place_recv.at[0])
+    places = jnp.sum(place_all[...].astype(F32), axis=1)
     named = jnp.where(places == b.astype(F32), 1.0, 0.0)
     count = jnp.broadcast_to(jnp.sum(named, axis=1, keepdims=True), (NB, TOK))
     below = (iota((NB, NB), 1) < iota((NB, NB), 0)).astype(BF16)
@@ -398,8 +331,131 @@
     sa[...] = jnp.where(q3 < 4.0, theirs, 0.0).reshape(NB * 8, TOK).astype(BF16)
     sb[...] = jnp.where(q3 < 4.0, 0.0, theirs).reshape(NB * 8, TOK).astype(BF16)
 
+    row_slot = jnp.where(named > 0.0, base + mm(named.astype(BF16), upper), -1.0)
+    row3 = iota((NB, MR, TOK), 1)
+    slot_lane3 = iota((NB, MR, TOK), 2)
+    row_slot = jnp.sum(jnp.where(row3 == slot_lane3, row_slot[:, None, :], 0.0), axis=2, keepdims=True)
+    vt[...] = jnp.where(row_slot == slot_lane3.astype(F32), 1.0, 0.0).reshape(NB * MR, TOK).astype(BF16)
+    fact = iota((TOK, NB * MR), 0)
+    row_id = iota((TOK, NB * MR), 1)
+    fact = jnp.where(fact == 0, row_id >> 5, jnp.where(fact == 1, row_id & 31, jnp.where(fact == 2, 1, 0)))
+    token_facts = mm(fact.astype(F32).astype(BF16), vt[...]).astype(BF16)
+
+    locals_[11].wait()
+    taken = iota((TOK, COLS), 0).astype(F32) < placed
+    text_only = jnp.where(taken, 0.0, text[...].astype(F32)).astype(BF16)
+    h_out[...] = mm(dmat[...], text_only).astype(BF16).reshape(NB, SLOT, COLS)
+    dispatch(h_out, h_in, a2a_send.at[1], set_recv.at[1])
+    info_out[...] = mm_nt(dmat[...], token_facts).astype(BF16).reshape(NB, SLOT, TOK)
+    dispatch(info_out, info_in, info_send.at[0], set_recv.at[2])
+
+
+    ci = iota((HALF, SET * SLOT), 0)
+    cj = iota((HALF, SET * SLOT), 1)
+    cmat[...] = jnp.where((ci == (cj >> 4) * CAPX + (cj & 15)) & ((cj & 15) < CAPX), 1.0, 0.0).astype(BF16)
+
+    def kv_arrive(xx, cc):
+        for yy in range(4):
+            block = blk_of((yh + yy) % 4, xx, cc)
+            wait_bytes(kvb.at[block], kv_recv.at[block])
+
+    def attend(state, xx, cc):
+        top, total, acc = state
+        block = jnp.concatenate([kvb[blk_of(yy, xx, cc)] for yy in range(4)], axis=1)
+        s = mm(qt, block)
+        new_top = jnp.maximum(top, jnp.max(s, axis=1, keepdims=True))
+        shrink = jnp.exp((top - new_top) * (HD ** -0.5))
+        w = jnp.exp((s - new_top) * (HD ** -0.5))
+        total = total * shrink + jnp.sum(w, axis=1, keepdims=True)
+        return new_top, total, acc * shrink + mm_nt(w.astype(BF16), block)
+
+    state = (jnp.full((TOK, 1), -1e30, F32), jnp.zeros((TOK, 1), F32), jnp.zeros((TOK, KVR), F32))
+    state = attend(state, x, core)
+    onward_core(kv_go, kvb, kv_recv, 1)
+    kv_arrive(x, 1 - core)
+    state = attend(state, x, 1 - core)
+    onward_core(kv_go, kvb, kv_recv, 3)
+    state = attend(state, (x + 3) % 4, core)
+    onward_core(kv_go, kvb, kv_recv, 2)
+    for which in range(2):
+        dispatch_wait(cot_in, set_recv.at[0], which)
+        xc[z, pl.ds(which * HALF, HALF), :] = packed(cot_in, which).astype(BF16)
+    cot_ring = ring_gather(xc, ring_send.at[0], ring_recv.at[0], 0, HALF)
+    next(cot_ring)
+    kv_arrive((x + 3) % 4, 1 - core)
+    state = attend(state, (x + 3) % 4, 1 - core)
+    state = attend(state, (x + 1) % 4, core)
+    kv_arrive((x + 1) % 4, 1 - core)
+    state = attend(state, (x + 1) % 4, 1 - core)
+    state = attend(state, (x + 2) % 4, core)
+    kv_arrive((x + 2) % 4, 1 - core)
+    _, total, acc = attend(state, (x + 2) % 4, 1 - core)
+    pick = (iota((HD, KVR), 1) == iota((HD, KVR), 0) + HD).astype(BF16)
+    attn = mm_nt(pick, (acc / total).astype(BF16))
+
+    def over_i(row):
+        row = row + pltpu.roll(row, 32, 1)
+        return row + pltpu.roll(row, 64, 1)
+
+    local_mean = over_i(jnp.broadcast_to(jnp.sum(attn, axis=0, keepdims=True), (8, TOK)))[0:1, :] * (1.0 / (4 * HD))
+    centred = attn - local_mean
+    squares = over_i(jnp.broadcast_to(jnp.sum(centred * centred, axis=0, keepdims=True), (8, TOK)))
+    st_all[e] = jnp.where(iota((8, TOK), 0) == 0, local_mean, squares)
+    to_experts(lambda to: st_all.at[e], st_all, e_send.at[1], e_recv.at[1])
+    scaled = centred * gain
+    left = jnp.concatenate([jnp.where(group == i, scaled, 0.0) for i in range(4)], axis=0).astype(BF16)
+
+    unit128 = (pi == pj).astype(BF16)
+    left = mm_nt(unit128, left).astype(BF16)
+
+    def merge_pair(j):
+        cols = pl.ds(pl.multiple_of(j * (2 * COLS), 2 * COLS), 2 * COLS)
+        v = mm(left, mw[:, cols])
+        v = (v[0:32] + v[32:64] + v[64:96] + v[96:128]).astype(BF16)
+        vp[2 * j] = v[:, 0:COLS]
+        vp[2 * j + 1] = v[:, COLS : 2 * COLS]
+
+    def merge_send(c, member):
+        send(vp.at[c], vp_all.at[e], e_send.at[2], e_recv.at[2], b, member * NZ + c)
+
+    def merge_others(i, carry):
+        j = (z // 2 + 1 + i) % 4
+        merge_pair(j)
+        for c in (2 * j, 2 * j + 1):
+            merge_send(c, 0)
+            merge_send(c, 1)
+        return carry
+
+    lax.fori_loop(0, 3, merge_others, 0)
+    merge_pair(z // 2)
+    merge_send(z + 1 - 2 * (z % 2), 0)
+    merge_send(z + 1 - 2 * (z % 2), 1)
+    merge_send(z, 1 - y)
+    vp_all[e] = vp[z]
+
+    next(cot_ring)
+
     cv_out[...] = (mm(ga[...], cot[:, 0:TOK]) + mm(gb[...], cot[:, TOK:COLS])).reshape(NB, 8, TOK)
     a2a_start(cv_out, cv_in, row_send.at[0], row_recv.at[0])
+
+    locals_[12].wait()
+    locals_[13].wait()
+
+    def gain_chunk(c, carry):
+        cols = pl.ds(pl.multiple_of(c * COLS, COLS), COLS)
+        g = ng_ref[:, cols]
+        wgs[:, cols] = (wg[:, cols].astype(F32) * g).astype(BF16)
+        wus[:, cols] = (wu[:, cols].astype(F32) * g).astype(BF16)
+        return carry
+
+    lax.fori_loop(0, NZ, gain_chunk, 0)
+
+    for which in range(2):
+        dispatch_wait(info_in, set_recv.at[2], which)
+        facts = packed(info_in, which)
+        row_of = facts[:, 0:1] * 32.0 + facts[:, 1:2] + (facts[:, 2:3] - 1.0)
+        hits = jnp.where(row_of == iota((HALF, NB * MR), 1).astype(F32), 1.0, 0.0)
+        pick_rows[which] = hits.astype(BF16)
 
     wait_bytes(gw_all.at[pl.ds(0, NE - 1)], e_recv.at[0])
     wait_bytes(st_all.at[pl.ds(0, NE - 1)], e_recv.at[1])
@@ -419,46 +475,27 @@
     )[0:MR]
     inv_column = jnp.sum(jnp.where(pi == pj, inv_std, 0.0), axis=1, keepdims=True)[0:MR]
     wait_bytes(vp_all.at[pl.ds(0, NE - 1)], e_recv.at[2])
-    next(cot_ring)
     vision = ((jnp.sum(vp_all[...].astype(F32), axis=0) + shift) * inv_column).astype(BF16)
     vis_all[z] = vision
-    fill = jnp.zeros((TOK - MR, COLS), BF16)
-    padded = jnp.concatenate([vision, fill], axis=0)
-    vi_out[...] = (mm(sa[...], padded[:, 0:TOK]) + mm(sb[...], padded[:, TOK:COLS])).reshape(NB, 8, TOK)
-    a2a_start(vi_out, vi_in, row_send.at[1], row_recv.at[1])
-    to_z(vis_all.at[z], vis_all, z_send.at[0], z_recv.at[0])
-
-    locals_[12].wait()
-    locals_[13].wait()
-
-    def gain_chunk(c, carry):
-        cols = pl.ds(pl.multiple_of(c * COLS, COLS), COLS)
-        g = ng_ref[:, cols]
-        wgs[:, cols] = (wg[:, cols].astype(F32) * g).astype(BF16)
-        wus[:, cols] = (wu[:, cols].astype(F32) * g).astype(BF16)
-        return carry
-
-    lax.fori_loop(0, NZ, gain_chunk, 0)
+    vblk[b] = vision
+    along_y(vi_go)
+
+    onward_x(vi_go, vblk, vi_recv)
+    for dx in (1, 3, 2):
+        onward_core(vi_go, vblk, vi_recv, dx)
     next(cot_ring)
     a2a_wait(cv_in, row_recv.at[0])
     cv = cv_in[...].reshape(NB * 8, TOK).astype(BF16)
     cv_all[z, :, 0:TOK] = mm_tn(sa[...], cv)[0:MR].astype(BF16)
     cv_all[z, :, TOK:COLS] = mm_tn(sb[...], cv)[0:MR].astype(BF16)
-    to_z(cv_all.at[z], cv_all, z_send.at[1], z_recv.at[1])
-
-    locals_[11].wait()
-    a2a_wait(vi_in, row_recv.at[1])
-    arrived = vi_in[...].reshape(NB * 8, TOK).astype(BF16)
-    taken = iota((TOK, TOK), 0).astype(F32) < placed
-    llm_a = jnp.where(taken, mm_tn(ga[...], arrived), text[:, 0:TOK].astype(F32))
-    llm_b = jnp.where(taken, mm_tn(gb[...], arrived), text[:, TOK:COLS].astype(F32))
-    text[:, 0:TOK] = llm_a.astype(BF16)
-    text[:, TOK:COLS] = llm_b.astype(BF16)
-    h_out[...] = mm(dmat[...], text[...]).astype(BF16).reshape(NB, SLOT, COLS)
-    dispatch(h_out, h_in, a2a_send.at[1], set_recv.at[1])
-
-    for _ in cot_ring:
-        pass
+
+    def vi_from_core(i, carry):
+        block = 2 * i + (1 - core)
+        wait_bytes(vblk.at[block], vi_recv.at[block])
+        return carry
+
+    lax.fori_loop(0, NB // 2, vi_from_core, 0)
+
     locals_[14].wait()
     act_grad[...] = jnp.zeros_like(act_grad)
     gate_acc[...] = jnp.zeros_like(gate_acc)
@@ -486,7 +523,8 @@
     def h_round(k, which):
         if k == 0:
             dispatch_wait(h_in, set_recv.at[1], which)
-            xh[z, pl.ds(which * HALF, HALF), :] = packed(h_in, which)
+            placed_rows = mm(pick_rows[which], vblk[...].reshape(NB * MR, COLS))
+            xh[z, pl.ds(which * HALF, HALF), :] = (packed(h_in, which) + placed_rows).astype(BF16)
         next(h_rings[which])
         project((z + k) % NZ, which)
         if 0 < k < 4:
@@ -525,18 +563,67 @@
         for ring in rings[which]:
             next(ring)
 
+    def place_grad(which):
+        rows = next(rings[which][0]).astype(BF16)
+        placed_grad = mm_tn(pick_rows[which], rows).reshape(NB, MR, COLS)
+        if which == 0:
+            by_row[...] = placed_grad
+        else:
+            by_row[...] = by_row[...] + placed_grad
+
     def give_back(which):
-        for j, (out, inn) in enumerate(((rg_out, rg_in), (dn_out, dn_in))):
-            rows = next(rings[which][j]).astype(BF16)
-            out[pl.ds(which * SET, SET)] = mm_tn(cmat[...], rows).astype(BF16).reshape(SET, SLOT, COLS)
-            if which == 1:
-                inn[b] = out[SET]
-            steps(which, -1, lambda i, to: send(out.at[i], inn.at[b], a2a_send.at[2 + j], a2a_recv.at[j], to, e))
+        rows = next(rings[which][1]).astype(BF16)
+        dn_out[pl.ds(which * SET, SET)] = mm_tn(cmat[...], rows).astype(BF16).reshape(SET, SLOT, COLS)
+        if which == 1:
+            dn_in[b] = dn_out[SET]
+        steps(which, -1, lambda i, to: send(dn_out.at[i], dn_in.at[b], a2a_send.at[2], a2a_recv.at[0], to, e))
+
+    def sum_over_cores():
+        for dx in (1, 3, 2, 0):
+            xx = lax.rem(x + dx, 4)
+            for yy in range(4):
+                core_out[xx, yy] = by_row[blk_of(yy, xx, 1 - core)].astype(BF16)
+            send(core_out.at[xx], core_in.at[xx], sum_send.at[0], core_recv.at[xx], blk_of(yh, x, 1 - core), e)
+
+    def sum_along_x():
+        for dx in (1, 3, 2, 0):
+            xx = lax.rem(x + dx, 4)
+            wait_bytes(core_in.at[xx], core_recv.at[xx])
+            for yy in range(4):
+                block = blk_of(yy, xx, core)
+                value = by_row[block] + core_in[xx, yy].astype(F32)
+                if dx > 0:
+                    x_out[dx - 1, yy] = value.astype(BF16)
+                else:
+                    by_row[block] = value
+            if dx > 0:
+                send(x_out.at[dx - 1], x_in.at[dx - 1], sum_send.at[1], x_recv.at[dx - 1], blk_of(yh, xx, core), e)
+
+    def sum_along_y():
+        for d in (0, 2, 1):
+            wait_bytes(x_in.at[d], x_recv.at[d])
+        for dy in (2, 1, 3, 0):
+            yy = lax.rem(yh + dy, 4)
+            block = blk_of(yy, x, core)
+            value = by_row[block]
+            for d in range(3):
+                value = value + x_in[d, yy].astype(F32)
+            if dy > 0:
+                y_out[dy - 1] = value.astype(BF16)
+                send(y_out.at[dy - 1], y_in.at[dy - 1], sum_send.at[2], y_recv.at[dy - 1], blk_of(yy, x, core), e)
+            else:
+                by_row[block] = value
 
     h_round(0, 0)
     h_round(0, 1)
+    next(cot_ring)
+    llm_in = jnp.where(taken, mm_tn(vt[...], vblk[...].reshape(NB * MR, COLS)), text[...].astype(F32))
+    text[...] = llm_in.astype(BF16)
+    h_round(1, 0)
+    h_round(1, 1)
+    next(cot_ring)
     lax.fori_loop(0, NZ, act_chunk, 0)
-    for k in range(1, 4):
+    for k in range(2, 4):
         h_round(k, 0)
         h_round(k, 1)
     h_round(4, 0)
@@ -546,16 +633,19 @@
     hidden_units(1)
     for which in (0, 1, 0, 1, 0, 1):
         reduce_round(which)
+    place_grad(0)
     give_back(0)
     reduce_round(1)
+    place_grad(1)
+    sum_over_cores()
     give_back(1)
-
-    a2a_wait(rg_in, a2a_recv.at[0])
-    token_grad = mm_tn(dmat[...], rg_in[...].reshape(NB * SLOT, COLS)).astype(BF16)
-    hg_out[...] = (mm(ga[...], token_grad[:, 0:TOK]) + mm(gb[...], token_grad[:, TOK:COLS])).reshape(NB, 8, TOK)
-    a2a_start(hg_out, hg_in, row_send.at[2], row_recv.at[2])
-
-    a2a_wait(dn_in, a2a_recv.at[1])
+    sum_along_x()
+    to_z(vis_all.at[z], vis_all, z_send.at[0], z_recv.at[0])
+    to_z(cv_all.at[z], cv_all, z_send.at[1], z_recv.at[1])
+
+    sum_along_y()
+
+    a2a_wait(dn_in, a2a_recv.at[0])
     dn = dn_in[...].reshape(NB * SLOT, COLS)
     mine_sum = mm_tn(dg_hi[...], dn) + mm_tn(dg_lo[...], dn)
     pair_out[...] = mine_sum.astype(BF16)
@@ -567,6 +657,12 @@
     def llm_cross(src):
         send(llm_all.at[src, own_half], llm_all.at[src, own_half], llm_send.at[1], llm_recv.at[1, src], b, other)
 
+    for d in range(3):
+        wait_bytes(y_in.at[d], y_recv.at[d])
+    row_grad = by_row[b] + (y_in[0].astype(F32) + y_in[1].astype(F32) + y_in[2].astype(F32))
+    hg_mine[...] = row_grad.astype(BF16)
+    send(hg_mine, hg_other, pair_send.at[1], pair_recv.at[1], b, other)
+
     wait_bytes(pair_in, pair_recv.at[0])
     layer = pair_out[own_half, :].astype(F32) + pair_in[...].astype(F32)
     llm_all[z, own_half, :] = (text[own_half, :].astype(F32) + layer).astype(BF16)
@@ -582,12 +678,10 @@
     for to in (2, 6, 1, 7):
         llm_along(z, to)
     llm_cross(z)
-    a2a_wait(hg_in, row_recv.at[2])
-    hg = hg_in[...].reshape(NB * 8, TOK).astype(BF16)
-    hg_mine[:, 0:TOK] = mm_tn(sa[...], hg)[0:MR].astype(BF16)
-    hg_mine[:, TOK:COLS] = mm_tn(sb[...], hg)[0:MR].astype(BF16)
-    hg_all[e] = hg_mine[...]
-    to_experts(lambda to: hg_mine, hg_all, e_send.at[3], e_recv.at[3])
+
+    wait_bytes(hg_other, pair_recv.at[1])
+    hg_all[z] = (hg_mine[...].astype(F32) + hg_other[...].astype(F32)).astype(BF16)
+    to_z(hg_all.at[z], hg_all, z_send.at[2], z_recv.at[2])
 
     for distance, onward in ((6, (1, 2)), (2, (7,)), (7, ()), (1, ()), (5, ()), (3, ()), (4, ())):
         src = llm_arrive(distance)
@@ -597,14 +691,14 @@
 
     wait_bytes(vis_all.at[pl.ds(0, NZ - 1)], z_recv.at[0])
     wait_bytes(cv_all.at[pl.ds(0, NZ - 1)], z_recv.at[1])
-    wait_bytes(hg_all.at[pl.ds(0, NE - 1)], e_recv.at[3])
+    wait_bytes(hg_all.at[pl.ds(0, NZ - 1)], z_recv.at[2])
 
     gw_sum = jnp.sum(gw_all[...], axis=0)
     ssq = jnp.zeros((MR, COLS), F32)
     cross = jnp.zeros((MR, COLS), F32)
     for c in range(NZ):
         v = vis_all[c].astype(F32)
-        ghg = (hg_all[c].astype(F32) + hg_all[NZ + c].astype(F32)) * ng_ref[:, c * COLS : (c + 1) * COLS]
+        ghg = hg_all[c].astype(F32) * ng_ref[:, c * COLS : (c + 1) * COLS]
         ssq = ssq + v * v
         cross = cross + ghg * v
     r = lax.rsqrt(jnp.sum(ssq, axis=1, keepdims=True) * (1.0 / WIDTH) + EPS)
@@ -614,7 +708,7 @@
     back_scaled = jnp.zeros((4 * HD, TOK), F32)
     for c in range(NZ):
         v = vis_all[c].astype(F32)
-        ghg = (hg_all[c].astype(F32) + hg_all[NZ + c].astype(F32)) * ng_ref[:, c * COLS : (c + 1) * COLS]
+        ghg = hg_all[c].astype(F32) * ng_ref[:, c * COLS : (c + 1) * COLS]
         vg = (cv_all[c].astype(F32) + (r * ghg - v * pull)).astype(BF16)
         wide = vg.astype(F32)
         dot_g = dot_g + wide * gw_sum[c : c + 1, :]
@@ -646,19 +740,24 @@
         llm_ref[:, c * COLS : (c + 1) * COLS] = llm_all[c]
 
     wait_bytes(kvb.at[pl.ds(0, NB - 1)], kv_send.at[0])
-    for index, buf in enumerate((cot_out, h_out, rg_out, dn_out)):
+    for index, buf in enumerate((cot_out, h_out, dn_out)):
         wait_bytes(buf.at[pl.ds(0, NB - 1)], a2a_send.at[index])
-    for index, buf in enumerate((cv_out, vi_out, hg_out)):
-        wait_bytes(buf.at[pl.ds(0, NB - 1)], row_send.at[index])
-    for index, buf in enumerate((gw_all, st_all, vp_all, hg_all)):
+    wait_bytes(vblk.at[pl.ds(0, NB - 1)], vi_send.at[0])
+    wait_bytes(info_out.at[pl.ds(0, NB - 1)], info_send.at[0])
+    wait_bytes(place_all.at[pl.ds(0, NB - 1)], info_send.at[1])
+    wait_bytes(cv_out.at[pl.ds(0, NB - 1)], row_send.at[0])
+    for index, buf in enumerate((core_out, x_out, y_out)):
+        wait_bytes(buf, sum_send.at[index])
+    for index, buf in enumerate((gw_all, st_all, vp_all)):
         wait_bytes(buf.at[pl.ds(0, NE - 1)], e_send.at[index])
-    for index, buf in enumerate((vis_all, cv_all)):
+    for index, buf in enumerate((vis_all, cv_all, hg_all)):
         wait_bytes(buf.at[pl.ds(0, NZ - 1)], z_send.at[index])
     wait_bytes(xc.at[pl.ds(0, NZ - 1)], ring_send.at[0])
     for index in range(2):
         wait_bytes(xh.at[pl.ds(0, NZ - 1), pl.ds(0, HALF)], ring_send.at[1 + index])
     wait_bytes(rs_out.at[:, pl.ds(0, 14)], rs_send.at[0])
     wait_bytes(pair_in, pair_send.at[0])
+    wait_bytes(hg_other, pair_send.at[1])
     wait_bytes(llm_all.at[pl.ds(0, NZ - 1), own_half], llm_send.at[0])
     wait_bytes(llm_all.at[:, own_half], llm_send.at[1])
 
@@ -666,8 +765,8 @@
 def scratch_shapes():
     V = pltpu.VMEM
     D = pltpu.SemaphoreType.DMA
-    routed = [V((NB, SLOT, COLS), BF16)] * 8
-    rows = [V((NB, 8, TOK), F32)] * 6
+    routed = [V((NB, SLOT, COLS), BF16)] * 6
+    rows = [V((NB, 8, TOK), F32)] * 2
     return (
         [V((HD, TOK), BF16)] * 3
         + [V((1, MR), jnp.int32), V((1, MR), jnp.int32), V((1, 4 * HD), F32), V((1, WIDTH), F32)]
@@ -679,15 +778,19 @@
         + [V((NB * SLOT, TOK), BF16)] * 3
         + [V((HALF, SET * SLOT), BF16)]
         + [V((NB * 8, TOK), BF16)] * 4
-        + routed + [D((4,)), D((2,)), D((2, 2))]
-        + rows + [D((3,)), D((3,))]
+        + routed + [D((3,)), D((1,)), D((3, 2))]
+        + [V((NB, MR, COLS), F32)] + [V((4, 4, MR, COLS), BF16)] * 2 + [V((3, 4, MR, COLS), BF16)] * 2
+        + [V((3, MR, COLS), BF16)] * 2 + [D((3,)), D((4,)), D((3,)), D((3,))]
+        + rows + [D((1,)), D((1,))]
+        + [V((NB, MR, COLS), BF16), D((1,)), D((NB,)), V((NB * MR, TOK), BF16), V((2, HALF, NB * MR), BF16)]
+        + [V((NB, SLOT, TOK), BF16)] * 2 + [D((2,)), V((NB, 1, TOK), jnp.int32), D((1,))]
         + [V((NE, NZ, COLS), F32), V((NE, 8, TOK), F32), V((NZ, MR, COLS), BF16), V((NE, MR, COLS), BF16)]
-        + [V((NE, MR, COLS), BF16), V((MR, COLS), BF16), D((4,)), D((4,))]
-        + [V((NZ, MR, COLS), BF16)] * 2 + [D((2,)), D((2,))]
+        + [V((NZ, MR, COLS), BF16), V((MR, COLS), BF16), V((MR, COLS), BF16), D((3,)), D((3,))]
+        + [V((NZ, MR, COLS), BF16)] * 2 + [D((3,)), D((3,))]
         + [V((NZ, ROWS, COLS), BF16)] * 2 + [D((3,)), D((3, 16))]
         + [V((ROWS, FG), F32), V((ROWS, FG), F32), V((ROWS, TOK), F32), V((ROWS, FG), F32), V((3, ROWS, FG), BF16)]
         + [V((4, 20, QUARTER, COLS), BF16)] * 2 + [D((1,)), D((4, 20))]
-        + [V((TOK, COLS), BF16), V((TOK // 2, COLS), BF16), D((1,)), D((1,))]
+        + [V((TOK, COLS), BF16), V((TOK // 2, COLS), BF16), D((2,)), D((2,))]
         + [V((NZ, TOK, COLS), BF16), D((2,)), D((2, NZ))]
     )
 

time: 139 us -> 134 us (0.964)
  Pallas kernels: 135 us -> 129 us
    pallas_call x1, Pallas kernels: 135 us -> 129 us  [body(): pl.pallas_call(kernel, out_shape=(jax.ShapeDtypeStruct((TOK, WIDTH), BF16...]
where the time goes in v4:
time: 134 us; the launch traced here: 133 us
  Pallas kernels  129 us (96%)
  local copies, waits for them, and re-layouts  3.27 us (2%)
    pallas_call x1, Pallas kernels, body(): pl.pallas_call(kernel, out_shape=(jax.ShapeDtypeStruct((TOK, WIDTH), BF16...  129 us
    unnamed x2, local copies, waits for them, and re-layouts  3.27 us

profile of v4, /device:TPU:1, one launch (start us, length us, event | category | flops | bytes accessed | tf_op | source)
XLA Modules:
  0.0 132.9 jit_solution(6726984407023214947)
XLA Ops:
  0.6 129.0 %shard_map.158 = (bf16[128,2048]{1,0:T(8,128)(2,1)}, f32[72,128]{1,0:T(8,128)}) custom-call(bf16[1,72,128]{2,1,0:T(8,128)(2,1)} %q_hbm.1, bf16[1,72,128]{2,1,0:T(8,128)(2,1)} %k_hbm.1, bf16[1,72,128]{2,1,0:T(8,128)(2,1)} %v_hbm.1, s32[1,32]{1,0:T(1,128)} %bitcast.10, s32[1,32]{1,0:T(1,128)} %bitcast.11, f32[1,288]{1,0:T(1,128)} %gain_hbm.1, ...), custom_call_target="tpu_custom_call" | custom-call | tf_op jit(solution)/shard_map/pallas_call | solution.py:804
  129.6 1.9 %copy.19 = bf16[128,2048]{1,0:T(8,128)(2,1)} copy(bf16[128,2048]{1,0:T(8,128)(2,1)} %get-tuple-element.8) | data formatting | bytes 1048576
  131.5 1.4 %copy.20 = f32[1,72,128]{2,1,0:T(8,128)} copy(f32[1,72,128]{2,1,0:T(8,128)} %bitcast.6) | data formatting | bytes 73728

commit v5 on v4

--- a/solution.py
+++ b/solution.py
@@ -60,7 +60,7 @@
     dmat, dg_hi, dg_lo, cmat, ga, gb, sa, sb,
     cot_out, cot_in, h_out, h_in, dn_out, dn_in, a2a_send, a2a_recv, set_recv,
     by_row, core_out, core_in, x_out, x_in, y_out, y_in, sum_send, core_recv, x_recv, y_recv,
-    cv_out, cv_in, row_send, row_recv, vblk, vi_send, vi_recv, vt, pick_rows, info_out, info_in, info_send, place_all, place_recv,
+    cv_out, cv_in, row_send, row_recv, vblk, vi_send, vi_recv, vt, pick_rows, pick_slots, info_out, info_in, info_send, place_all, place_recv,
     gw_all, st_all, vp, vp_all, hg_all, hg_mine, hg_other, e_send, e_recv,
     vis_all, cv_all, z_send, z_recv,
     xc, xh, ring_send, ring_recv,
@@ -311,6 +311,24 @@
 
     onward_x(kv_go, kvb, kv_recv)
 
+    def kv_arrive(xx, cc):
+        for yy in range(4):
+            block = blk_of((yh + yy) % 4, xx, cc)
+            wait_bytes(kvb.at[block], kv_recv.at[block])
+
+    def attend(state, xx, cc):
+        top, total, acc = state
+        block = jnp.concatenate([kvb[blk_of(yy, xx, cc)] for yy in range(4)], axis=1)
+        s = mm(qt, block)
+        new_top = jnp.maximum(top, jnp.max(s, axis=1, keepdims=True))
+        shrink = jnp.exp((top - new_top) * (HD ** -0.5))
+        w = jnp.exp((s - new_top) * (HD ** -0.5))
+        total = total * shrink + jnp.sum(w, axis=1, keepdims=True)
+        return new_top, total, acc * shrink + mm_nt(w.astype(BF16), block)
+
+    state = (jnp.full((TOK, 1), -1e30, F32), jnp.zeros((TOK, 1), F32), jnp.zeros((TOK, KVR), F32))
+    state = attend(state, x, core)
+
     wait_bytes(place_all.at[pl.ds(0, NB - 1)], place_recv.at[0])
     places = jnp.sum(place_all[...].astype(F32), axis=1)
     named = jnp.where(places == b.astype(F32), 1.0, 0.0)
@@ -354,23 +372,6 @@
     cj = iota((HALF, SET * SLOT), 1)
     cmat[...] = jnp.where((ci == (cj >> 4) * CAPX + (cj & 15)) & ((cj & 15) < CAPX), 1.0, 0.0).astype(BF16)
 
-    def kv_arrive(xx, cc):
-        for yy in range(4):
-            block = blk_of((yh + yy) % 4, xx, cc)
-            wait_bytes(kvb.at[block], kv_recv.at[block])
-
-    def attend(state, xx, cc):
-        top, total, acc = state
-        block = jnp.concatenate([kvb[blk_of(yy, xx, cc)] for yy in range(4)], axis=1)
-        s = mm(qt, block)
-        new_top = jnp.maximum(top, jnp.max(s, axis=1, keepdims=True))
-        shrink = jnp.exp((top - new_top) * (HD ** -0.5))
-        w = jnp.exp((s - new_top) * (HD ** -0.5))
-        total = total * shrink + jnp.sum(w, axis=1, keepdims=True)
-        return new_top, total, acc * shrink + mm_nt(w.astype(BF16), block)
-
-    state = (jnp.full((TOK, 1), -1e30, F32), jnp.zeros((TOK, 1), F32), jnp.zeros((TOK, KVR), F32))
-    state = attend(state, x, core)
     onward_core(kv_go, kvb, kv_recv, 1)
     kv_arrive(x, 1 - core)
     state = attend(state, x, 1 - core)
@@ -456,6 +457,10 @@
         row_of = facts[:, 0:1] * 32.0 + facts[:, 1:2] + (facts[:, 2:3] - 1.0)
         hits = jnp.where(row_of == iota((HALF, NB * MR), 1).astype(F32), 1.0, 0.0)
         pick_rows[which] = hits.astype(BF16)
+        across = mm_nt(unit128, facts.astype(BF16))
+        row_of = across[0:1, :] * 32.0 + across[1:2, :] + (across[2:3, :] - 1.0)
+        hits = jnp.where(row_of == iota((NB * MR, HALF), 0).astype(F32), 1.0, 0.0)
+        pick_slots[which] = hits.astype(BF16)
 
     wait_bytes(gw_all.at[pl.ds(0, NE - 1)], e_recv.at[0])
     wait_bytes(st_all.at[pl.ds(0, NE - 1)], e_recv.at[1])
@@ -481,9 +486,10 @@
     along_y(vi_go)
 
     onward_x(vi_go, vblk, vi_recv)
-    for dx in (1, 3, 2):
-        onward_core(vi_go, vblk, vi_recv, dx)
+    onward_core(vi_go, vblk, vi_recv, 1)
     next(cot_ring)
+    onward_core(vi_go, vblk, vi_recv, 3)
+    onward_core(vi_go, vblk, vi_recv, 2)
     a2a_wait(cv_in, row_recv.at[0])
     cv = cv_in[...].reshape(NB * 8, TOK).astype(BF16)
     cv_all[z, :, 0:TOK] = mm_tn(sa[...], cv)[0:MR].astype(BF16)
@@ -526,6 +532,8 @@
             placed_rows = mm(pick_rows[which], vblk[...].reshape(NB * MR, COLS))
             xh[z, pl.ds(which * HALF, HALF), :] = (packed(h_in, which) + placed_rows).astype(BF16)
         next(h_rings[which])
+
+    def h_project(k, which):
         project((z + k) % NZ, which)
         if 0 < k < 4:
             project((z + 8 - k) % NZ, which)
@@ -565,7 +573,7 @@
 
     def place_grad(which):
         rows = next(rings[which][0]).astype(BF16)
-        placed_grad = mm_tn(pick_rows[which], rows).reshape(NB, MR, COLS)
+        placed_grad = mm(pick_slots[which], rows).reshape(NB, MR, COLS)
         if which == 0:
             by_row[...] = placed_grad
         else:
@@ -614,22 +622,24 @@
             else:
                 by_row[block] = value
 
-    h_round(0, 0)
-    h_round(0, 1)
-    next(cot_ring)
-    llm_in = jnp.where(taken, mm_tn(vt[...], vblk[...].reshape(NB * MR, COLS)), text[...].astype(F32))
-    text[...] = llm_in.astype(BF16)
-    h_round(1, 0)
-    h_round(1, 1)
-    next(cot_ring)
-    lax.fori_loop(0, NZ, act_chunk, 0)
-    for k in range(2, 4):
+    for k in range(4):
         h_round(k, 0)
         h_round(k, 1)
+        h_project(k, 0)
+        h_project(k, 1)
+        if k < 2:
+            next(cot_ring)
+        if k == 0:
+            llm_in = jnp.where(taken, mm_tn(vt[...], vblk[...].reshape(NB * MR, COLS)), text[...].astype(F32))
+            text[...] = llm_in.astype(BF16)
+        if k > 1:
+            lax.fori_loop((k - 2) * (NZ // 2), (k - 1) * (NZ // 2), act_chunk, 0)
     h_round(4, 0)
+    h_project(4, 0)
     hidden_units(0)
     reduce_round(0)
     h_round(4, 1)
+    h_project(4, 1)
     hidden_units(1)
     for which in (0, 1, 0, 1, 0, 1):
         reduce_round(which)
@@ -644,7 +654,6 @@
     to_z(cv_all.at[z], cv_all, z_send.at[1], z_recv.at[1])
 
     sum_along_y()
-
     a2a_wait(dn_in, a2a_recv.at[0])
     dn = dn_in[...].reshape(NB * SLOT, COLS)
     mine_sum = mm_tn(dg_hi[...], dn) + mm_tn(dg_lo[...], dn)
@@ -657,12 +666,6 @@
     def llm_cross(src):
         send(llm_all.at[src, own_half], llm_all.at[src, own_half], llm_send.at[1], llm_recv.at[1, src], b, other)
 
-    for d in range(3):
-        wait_bytes(y_in.at[d], y_recv.at[d])
-    row_grad = by_row[b] + (y_in[0].astype(F32) + y_in[1].astype(F32) + y_in[2].astype(F32))
-    hg_mine[...] = row_grad.astype(BF16)
-    send(hg_mine, hg_other, pair_send.at[1], pair_recv.at[1], b, other)
-
     wait_bytes(pair_in, pair_recv.at[0])
     layer = pair_out[own_half, :].astype(F32) + pair_in[...].astype(F32)
     llm_all[z, own_half, :] = (text[own_half, :].astype(F32) + layer).astype(BF16)
@@ -679,15 +682,25 @@
         llm_along(z, to)
     llm_cross(z)
 
-    wait_bytes(hg_other, pair_recv.at[1])
-    hg_all[z] = (hg_mine[...].astype(F32) + hg_other[...].astype(F32)).astype(BF16)
-    to_z(hg_all.at[z], hg_all, z_send.at[2], z_recv.at[2])
-
-    for distance, onward in ((6, (1, 2)), (2, (7,)), (7, ()), (1, ()), (5, ()), (3, ()), (4, ())):
+    for d in range(3):
+        wait_bytes(y_in.at[d], y_recv.at[d])
+    row_grad = by_row[b] + (y_in[0].astype(F32) + y_in[1].astype(F32) + y_in[2].astype(F32))
+    hg_mine[...] = row_grad.astype(BF16)
+    send(hg_mine, hg_other, pair_send.at[1], pair_recv.at[1], b, other)
+
+    def llm_onward(distance, onward):
         src = llm_arrive(distance)
         for to in onward:
             llm_along(src, to)
         llm_cross(src)
+
+    llm_onward(6, (1, 2))
+    llm_onward(2, (7,))
+    wait_bytes(hg_other, pair_recv.at[1])
+    hg_all[z] = (hg_mine[...].astype(F32) + hg_other[...].astype(F32)).astype(BF16)
+    to_z(hg_all.at[z], hg_all, z_send.at[2], z_recv.at[2])
+    for distance in (7, 1, 5, 3, 4):
+        llm_onward(distance, ())
 
     wait_bytes(vis_all.at[pl.ds(0, NZ - 1)], z_recv.at[0])
     wait_bytes(cv_all.at[pl.ds(0, NZ - 1)], z_recv.at[1])
@@ -782,7 +795,7 @@
         + [V((NB, MR, COLS), F32)] + [V((4, 4, MR, COLS), BF16)] * 2 + [V((3, 4, MR, COLS), BF16)] * 2
         + [V((3, MR, COLS), BF16)] * 2 + [D((3,)), D((4,)), D((3,)), D((3,))]
         + rows + [D((1,)), D((1,))]
-        + [V((NB, MR, COLS), BF16), D((1,)), D((NB,)), V((NB * MR, TOK), BF16), V((2, HALF, NB * MR), BF16)]
+        + [V((NB, MR, COLS), BF16), D((1,)), D((NB,)), V((NB * MR, TOK), BF16), V((2, HALF, NB * MR), BF16), V((2, NB * MR, HALF), BF16)]
         + [V((NB, SLOT, TOK), BF16)] * 2 + [D((2,)), V((NB, 1, TOK), jnp.int32), D((1,))]
         + [V((NE, NZ, COLS), F32), V((NE, 8, TOK), F32), V((NZ, MR, COLS), BF16), V((NE, MR, COLS), BF16)]
         + [V((NZ, MR, COLS), BF16), V((MR, COLS), BF16), V((MR, COLS), BF16), D((3,)), D((3,))]

time: 134 us -> 133 us (level); the launches traced: 133 us -> 130 us
  Pallas kernels: 129 us -> 126 us
    pallas_call x1, Pallas kernels: 129 us -> 126 us  [body(): pl.pallas_call(kernel, out_shape=(jax.ShapeDtypeStruct((TOK, WIDTH), BF16...]
where the time goes in v5:
time: 133 us; the launch traced here: 130 us
  Pallas kernels  126 us (95%)
  local copies, waits for them, and re-layouts  3.27 us (2%)
    pallas_call x1, Pallas kernels, body(): pl.pallas_call(kernel, out_shape=(jax.ShapeDtypeStruct((TOK, WIDTH), BF16...  126 us
    unnamed x2, local copies, waits for them, and re-layouts  3.27 us

profile of v5, /device:TPU:1, one launch (start us, length us, event | category | flops | bytes accessed | tf_op | source)
XLA Modules:
  0.0 130.4 jit_solution(619830436643092570)
XLA Ops:
  0.6 126.5 %shard_map.158 = (bf16[128,2048]{1,0:T(8,128)(2,1)}, f32[72,128]{1,0:T(8,128)}) custom-call(bf16[1,72,128]{2,1,0:T(8,128)(2,1)} %q_hbm.1, bf16[1,72,128]{2,1,0:T(8,128)(2,1)} %k_hbm.1, bf16[1,72,128]{2,1,0:T(8,128)(2,1)} %v_hbm.1, s32[1,32]{1,0:T(1,128)} %bitcast.10, s32[1,32]{1,0:T(1,128)} %bitcast.11, f32[1,288]{1,0:T(1,128)} %gain_hbm.1, ...), custom_call_target="tpu_custom_call" | custom-call | tf_op jit(solution)/shard_map/pallas_call | solution.py:817
  127.1 1.9 %copy.19 = bf16[128,2048]{1,0:T(8,128)(2,1)} copy(bf16[128,2048]{1,0:T(8,128)(2,1)} %get-tuple-element.8) | data formatting | bytes 1048576
  129.0 1.4 %copy.20 = f32[1,72,128]{2,1,0:T(8,128)} copy(f32[1,72,128]{2,1,0:T(8,128)} %bitcast.6) | data formatting | bytes 73728
